TPU v7x, 128 devices: a whole 4x4x4 slice. The times are simulated.
128 devices in a mesh: dp: 16 (over y_lo, x, core), proto: 8 (over z, y_hi).
Axes of the slice: x: 4, y: 4 (y_hi: 2, y_lo: 2; y = y_hi * 2 + y_lo), z: 4, core: 2. Of those that a mesh axis runs over, the one named last changes fastest.
Arguments:
- teacher_feats: bfloat16 [4096, 256], P('dp')
- student_feats: bfloat16 [4096, 256], P('dp')
- proto_weight: bfloat16 [256, 262144], P(None, 'proto')
Outputs:
- feature_grad: float32 [4096, 256], P('dp')
- proto_grad: float32 [256, 262144], P('dp', 'proto')
All inputs are finite; a program needn't handle non-finite values.
Results may differ from a plain program's by a relative error of at most 0.0003.
The roundings to bfloat16 on the way count: a program that leaves them out, or rounds other values in their place, can miss the bound.
Values may be sent and summed in bfloat16 or wider, within the bound.
No kernel may reach another device: no remote copies, remote signals or barrier semaphores. Data moves between devices by JAX's collectives and lax.ppermute only.
A program may use at most 256 MiB of HBM per device.

v0:
```python
import functools
import math

import jax
import jax.numpy as jnp
import numpy as np
from jax import lax
from jax.experimental import pallas as pl
from jax.experimental.pallas import tpu as pltpu
from jax.sharding import PartitionSpec as P

ITERS = 3
EPS = 1e-06
TEACH = float(np.float32(0.07))
STUD = float(np.float32(0.1))
LOG2E = math.log2(math.e)
TSCALE = LOG2E / TEACH
SSCALE = LOG2E / STUD
LOG_INV = -math.log2(STUD)
F32 = jnp.float32
BF16 = jnp.bfloat16
LANES = 128
MIB = 1024 * 1024
AXES = ("yl", "x", "c", "z", "yh")
DP = ("yl", "x", "c")
PROTO = ("z", "yh")
CHIPS = ("yl", "x")
PLANE = ("yl", "x", "yh")
PILLAR = ("z", "c")


def unit_rows(feats):
    wide = feats.astype(F32)
    squares = jnp.sum(wide * wide, axis=1, keepdims=True)
    return (wide * lax.rsqrt(squares + EPS)).astype(BF16)


def dot(a, b):
    return jnp.dot(a, b, preferred_element_type=F32)


def dot_nt(a, b):
    return lax.dot_general(a, b, (((1,), (1,)), ((), ())), preferred_element_type=F32)


def fold_rows(value):
    return jnp.sum(value.reshape(value.shape[0] // 8, 8, value.shape[1]), axis=0)


def params(mib):
    return pltpu.CompilerParams(vmem_limit_bytes=mib * MIB)


def vmem():
    return pl.BlockSpec(memory_space=pltpu.VMEM)


def smem():
    return pl.BlockSpec(memory_space=pltpu.SMEM)


def block_of(near_ref, far_ref, block):
    pairs = near_ref.shape[0]
    return near_ref[block] if block < pairs else far_ref[block - pairs]


def places(core, pairs, per):
    found = []
    for block in range(2 * pairs):
        parity = core if block < pairs else 1 - core
        found += [(2 * (block % pairs) + parity) * per + part for part in range(per)]
    return found


def sweep_kernel(copies, tile, has_parts, has_extra, *refs):
    refs = list(refs)
    core = refs.pop(0)[0]
    parts_ref = refs.pop(0) if has_parts else None
    extra_ref = refs.pop(0) if has_extra else None
    protos_ref, near_ref, far_ref, col_ref, out_ref, sums, scale, kern, acc = refs
    pairs, rows, _ = near_ref.shape
    blocks = 2 * pairs
    per = rows // LANES
    groups = blocks * per
    placed = places(core, pairs, per)
    if has_parts:
        sums[...] = 1.0 / jnp.sum(parts_ref[...], axis=0)
        for at, place in enumerate(placed):
            scale[at : at + 1, :] = sums[pl.ds(place, 1), :]
    acc[...] = jnp.zeros_like(acc)

    def one_tile(step, carry):
        here = pl.ds(pl.multiple_of(step * tile, tile), tile)
        protos = protos_ref[here, :]
        col_acc = jnp.zeros((tile, LANES), F32)
        for block in range(blocks):
            logits = dot_nt(protos, block_of(near_ref, far_ref, block))
            for part in range(per):
                value = jnp.exp2(logits[:, part * LANES : (part + 1) * LANES] * TSCALE)
                at = block * per + part
                kern[:, at * LANES : (at + 1) * LANES] = value
                col_acc = col_acc + (value * scale[at : at + 1, :] if has_parts else value)
        col = 1.0 / jnp.sum(col_acc, axis=1, keepdims=True)
        wide_col = jnp.broadcast_to(col, (tile, LANES))
        col_ref[here, :] = wide_col
        for at in range(groups):
            lanes = slice(at * LANES, (at + 1) * LANES)
            acc[:, lanes] += fold_rows(kern[:, lanes] * wide_col)
        return carry

    lax.fori_loop(0, protos_ref.shape[0] // tile, one_tile, 0)
    for at, place in enumerate(placed):
        total = jnp.sum(acc[:, at * LANES : (at + 1) * LANES], axis=0, keepdims=True)
        for copy in range(copies):
            out_ref[copy, pl.ds(place, 1), :] = total
    if has_extra:
        extra = extra_ref[...]
        for copy in range(copies):
            out_ref[copy, groups:, :] = extra


def sweep(core, parts, extra, protos, near, far, copies, tile=256):
    count = protos.shape[0]
    pairs, rows, _ = near.shape
    total = 2 * pairs * rows
    groups = total // LANES
    sent = groups if extra is None else groups + extra.shape[0]
    args = [a for a in (parts, extra) if a is not None] + [protos, near, far]
    return pl.pallas_call(
        functools.partial(sweep_kernel, copies, tile, parts is not None, extra is not None),
        in_specs=[smem()] + [vmem()] * len(args),
        out_specs=[vmem()] * 2,
        out_shape=[
            jax.ShapeDtypeStruct((count, LANES), F32),
            jax.ShapeDtypeStruct((copies, sent, LANES), F32),
        ],
        scratch_shapes=[
            pltpu.VMEM((groups, LANES), F32),
            pltpu.VMEM((groups, LANES), F32),
            pltpu.VMEM((tile, total), F32),
            pltpu.VMEM((8, total), F32),
        ],
        compiler_params=params(24),
        name="sweep",
    )(core, *args)


def totals_kernel(tile, core_ref, protos_ref, near_ref, far_ref, out_ref, acc):
    acc[...] = jnp.zeros_like(acc)
    pairs, rows, _ = near_ref.shape
    blocks = 2 * pairs

    def one_tile(step, carry):
        protos = protos_ref[pl.ds(pl.multiple_of(step * tile, tile), tile), :]
        for block in range(blocks):
            logits = dot_nt(protos, block_of(near_ref, far_ref, block))
            acc[:, block * rows : (block + 1) * rows] += fold_rows(jnp.exp2(logits * SSCALE))
        return carry

    lax.fori_loop(0, protos_ref.shape[0] // tile, one_tile, 0)
    for at, place in enumerate(places(core_ref[0], pairs, rows // LANES)):
        out_ref[pl.ds(place, 1), :] = jnp.sum(
            acc[:, at * LANES : (at + 1) * LANES], axis=0, keepdims=True
        )


def totals(core, protos, near, far, tile=512):
    count, depth = protos.shape
    pairs, rows, _ = near.shape
    blocks = 2 * pairs
    groups = blocks * rows // LANES
    return pl.pallas_call(
        functools.partial(totals_kernel, tile),
        in_specs=[smem()] + [vmem()] * 3,
        out_specs=vmem(),
        out_shape=jax.ShapeDtypeStruct((groups, LANES), F32),
        scratch_shapes=[pltpu.VMEM((8, blocks * rows), F32)],
        compiler_params=params(24),
        cost_estimate=pl.CostEstimate(
            flops=2 * count * depth * blocks * rows,
            bytes_accessed=4 * MIB,
            transcendentals=count * blocks * rows,
        ),
        name="totals",
    )(core, protos, near, far)


def hop_kernel(copies, in_ref, out_ref):
    total = jnp.sum(in_ref[...], axis=0)
    for copy in range(copies):
        out_ref[copy] = total


def hop(parts, copies):
    return pl.pallas_call(
        functools.partial(hop_kernel, copies),
        in_specs=[vmem()],
        out_specs=vmem(),
        out_shape=jax.ShapeDtypeStruct((copies,) + parts.shape[1:], F32),
        compiler_params=params(4),
        name="hop",
    )(parts)


def exchange(parts, axes):
    return lax.all_to_all(parts, axes, 0, 0, tiled=True)


def spread(parts, pillar):
    return exchange(hop(exchange(parts, PLANE), pillar), PILLAR)


def diff_kernel(
    tile, core_ref, parts_ref, col_ref, protos_ref, cols_ref, near_ref, far_ref, stud_near_ref, stud_far_ref,
    out_ref, mine_ref, other_ref, all_sums, scale, norm, diff, sems,
):
    pairs, rows, _ = near_ref.shape
    blocks = 2 * pairs
    per = rows // LANES
    groups = blocks * per
    all_sums[...] = LOG_INV - jnp.log2(jnp.sum(parts_ref[...], axis=0))
    for at, place in enumerate(places(core_ref[0], pairs, per)):
        scale[at : at + 1, :] = all_sums[pl.ds(place, 1), :]
        norm[at : at + 1, :] = all_sums[pl.ds(groups + place, 1), :]
    tiles = protos_ref.shape[0] // tile

    def span(step):
        return pl.ds(pl.multiple_of(step * tile, tile), tile)

    def store(step):
        return pltpu.make_async_copy(diff.at[span(step), :], out_ref.at[span(step), :], sems.at[step])

    def one_tile(step, carry):
        here = span(step)
        log_col = jnp.log2(col_ref[here, :])
        for block in range(blocks):
            teach_logits = dot_nt(protos_ref[here, :], block_of(near_ref, far_ref, block))
            stud_logits = dot_nt(protos_ref[here, :], block_of(stud_near_ref, stud_far_ref, block))
            for part in range(per):
                at = block * per + part
                lanes = slice(part * LANES, (part + 1) * LANES)
                target = jnp.exp2(teach_logits[:, lanes] * TSCALE + (scale[at : at + 1, :] + log_col))
                prob = jnp.exp2(stud_logits[:, lanes] * SSCALE + norm[at : at + 1, :])
                diff[here, at * LANES : (at + 1) * LANES] = (prob - target).astype(BF16)
        store(step).start()
        return carry

    lax.fori_loop(0, tiles, one_tile, 0)

    def one_pair(pair, carry):
        for first, ref in ((0, mine_ref), (pairs, other_ref)):
            start = pl.multiple_of((pair + first) * rows, rows)
            ref[pair] = dot(cols_ref[...], diff[:, pl.ds(start, rows)])
        return carry

    lax.fori_loop(0, pairs, one_pair, 0)

    def finish(step, carry):
        store(step).wait()
        return carry

    lax.fori_loop(0, tiles, finish, 0)


def differences(core, parts, col, protos, cols, near, far, stud_near, stud_far, tile=512):
    count, depth = protos.shape
    pairs, rows, _ = near.shape
    blocks = 2 * pairs
    groups = blocks * rows // LANES
    return pl.pallas_call(
        functools.partial(diff_kernel, tile),
        in_specs=[smem()] + [vmem()] * 8,
        out_specs=[pl.BlockSpec(memory_space=pl.ANY)] + [vmem()] * 2,
        out_shape=[
            jax.ShapeDtypeStruct((count, blocks * rows), BF16),
            jax.ShapeDtypeStruct((pairs, depth, rows), F32),
            jax.ShapeDtypeStruct((pairs, depth, rows), F32),
        ],
        scratch_shapes=[
            pltpu.VMEM((2 * groups, LANES), F32),
            pltpu.VMEM((groups, LANES), F32),
            pltpu.VMEM((groups, LANES), F32),
            pltpu.VMEM((count, blocks * rows), BF16),
            pltpu.SemaphoreType.DMA((count // tile,)),
        ],
        compiler_params=params(40),
        name="differences",
    )(core, parts, col, protos, cols, near, far, stud_near, stud_far)


SPAN = 250.0
FLOOR = 125.0


def power_of(top):
    return jnp.minimum(jnp.ceil(jnp.log2(jnp.maximum(top, 2.0**-120))), 126.0)


def encode(values, power):
    size = jnp.exp2(jnp.minimum(jnp.abs(values) * jnp.exp2(-power), 1.0) * SPAN - FLOOR)
    return jnp.where(values < 0, -size, size).astype(BF16)


def decode(code, power):
    wide = code.astype(F32)
    size = (jnp.log2(jnp.abs(wide)) + FLOOR) * (1.0 / SPAN) * jnp.exp2(power)
    return jnp.where(wide < 0, -size, size)


def decode_kernel(code_ref, out_ref):
    sources, share, width = code_ref.shape
    count = out_ref.shape[1] // sources

    def one_source(source, carry):
        powers = code_ref[source, :, count:].astype(F32)
        for part in range(count // LANES):
            code = code_ref[source, :, part * LANES : (part + 1) * LANES]
            start = pl.multiple_of(source * count + part * LANES, LANES)
            out_ref[:, pl.ds(start, LANES)] = decode(code, powers[part : part + 1, :])
        return carry

    lax.fori_loop(0, sources, one_source, 0)


def decoded(codes):
    sources, share, width = codes.shape
    return pl.pallas_call(
        decode_kernel,
        in_specs=[vmem()],
        out_specs=vmem(),
        out_shape=jax.ShapeDtypeStruct((share, sources * (width - LANES)), F32),
        compiler_params=params(16),
        cost_estimate=pl.CostEstimate(flops=16 * sources * share * width, bytes_accessed=4 * MIB, transcendentals=0),
        name="decoded",
    )(codes)


def pgrad_kernel(tile, diff_ref, near_ref, far_ref, out_ref, diff, powers, sems):
    tiles = diff.shape[0] // tile
    pairs, rows, depth = near_ref.shape
    reach = pairs * rows
    dests, share, _ = out_ref.shape

    def span(step):
        return pl.ds(pl.multiple_of(step * tile, tile), tile)

    def load(step):
        return pltpu.make_async_copy(diff_ref.at[span(step), :], diff.at[span(step), :], sems.at[step])

    def begin(step, carry):
        load(step).start()
        return carry

    def one_tile(step, carry):
        load(step).wait()
        mine = dot(diff[span(step), :reach], near_ref[...].reshape(reach, depth))
        others = dot(diff[span(step), reach:], far_ref[...].reshape(reach, depth))
        grads = (4096.0 * (mine + others)).T
        for dest in range(dests):
            values = grads[dest * share : (dest + 1) * share, :]
            power = power_of(jnp.max(jnp.abs(values), axis=0, keepdims=True))
            out_ref[dest, :, span(step)] = encode(values, power)
            for part in range(tile // LANES):
                row = step * (tile // LANES) + part
                powers[dest, pl.ds(row, 1), :] = power[:, part * LANES : (part + 1) * LANES]
        return carry

    lax.fori_loop(0, tiles, begin, 0)
    lax.fori_loop(0, tiles, one_tile, 0)
    out_ref[:, :, diff.shape[0] :] = powers[...].astype(BF16)


def proto_part(diff, near, far, dests, tile=512):
    count, total = diff.shape
    depth = near.shape[2]
    return pl.pallas_call(
        functools.partial(pgrad_kernel, tile),
        in_specs=[pl.BlockSpec(memory_space=pl.ANY), vmem(), vmem()],
        out_specs=vmem(),
        out_shape=jax.ShapeDtypeStruct((dests, depth // dests, count + LANES), BF16),
        scratch_shapes=[
            pltpu.VMEM((count, total), BF16),
            pltpu.VMEM((dests, count // LANES, LANES), F32),
            pltpu.SemaphoreType.DMA((count // tile,)),
        ],
        compiler_params=params(56),
        cost_estimate=pl.CostEstimate(
            flops=2 * count * total * depth, bytes_accessed=20 * MIB, transcendentals=0
        ),
        name="proto_part",
    )(diff, near, far)


GROUP = 16


def cut_kernel(level_ref, mine_ref, given_ref, own_ref, *code_refs):
    quarter = own_ref.shape[1]
    for by in range(len(code_refs) + 1):
        start = pl.multiple_of(lax.rem(level_ref[0] + by, len(code_refs) + 1) * quarter, quarter)
        for pair in range(own_ref.shape[0]):
            values = mine_ref[pair, pl.ds(start, quarter), :] + given_ref[pair, pl.ds(start, quarter), :]
            if by == 0:
                own_ref[pair] = values
                continue
            parts = [values[at : at + GROUP] for at in range(0, quarter, GROUP)]
            power = power_of(functools.reduce(jnp.maximum, [jnp.abs(part) for part in parts]))
            for at, part in enumerate(parts):
                code_refs[by - 1][pair, at * GROUP : (at + 1) * GROUP, :] = encode(part, power)
            code_refs[by - 1][pair, quarter:, :] = power.astype(BF16)


def cuts(level, mine, given, levels):
    pairs, depth, rows = mine.shape
    quarter = depth // levels
    return pl.pallas_call(
        cut_kernel,
        in_specs=[smem(), vmem(), vmem()],
        out_specs=[vmem()] * levels,
        out_shape=[jax.ShapeDtypeStruct((pairs, quarter, rows), F32)]
        + [jax.ShapeDtypeStruct((pairs, quarter + GROUP, rows), BF16)] * (levels - 1),
        compiler_params=params(16),
        name="cuts",
    )(level, mine, given)


def join_kernel(own_ref, *refs):
    out_ref = refs[-1]
    quarter = own_ref.shape[1]
    for pair in range(own_ref.shape[0]):
        powers = [ref[pair, quarter:, :].astype(F32) for ref in refs[:-1]]
        for at in range(0, quarter, GROUP):
            total = own_ref[pair, at : at + GROUP, :]
            for ref, power in zip(refs[:-1], powers):
                total = total + decode(ref[pair, at : at + GROUP, :], power)
            out_ref[pair, at : at + GROUP, :] = total


def joined(own, codes):
    return pl.pallas_call(
        join_kernel,
        in_specs=[vmem()] * (1 + len(codes)),
        out_specs=vmem(),
        out_shape=jax.ShapeDtypeStruct(own.shape, F32),
        compiler_params=params(8),
        name="joined",
    )(own, *codes)


def protos_kernel(place_ref, weight_ref, cols_ref, protos_ref, held, sem):
    depth, count = cols_ref.shape
    start = pl.multiple_of(place_ref[0] * count, count)
    copy = pltpu.make_async_copy(weight_ref.at[:, pl.ds(start, count)], held, sem)
    copy.start()
    copy.wait()
    tile = 512
    for at in range(0, count, tile):
        wide = held[:, at : at + tile].astype(F32)
        squares = jnp.sum(wide * wide, axis=0, keepdims=True)
        unit = wide * lax.rsqrt(squares + EPS)
        cols_ref[:, at : at + tile] = unit.astype(BF16)
        protos_ref[at : at + tile, :] = unit.T.astype(BF16)


def unit_protos(place, weight, count):
    depth = weight.shape[0]
    return pl.pallas_call(
        protos_kernel,
        in_specs=[smem(), pl.BlockSpec(memory_space=pl.ANY)],
        out_specs=[vmem()] * 2,
        out_shape=[
            jax.ShapeDtypeStruct((depth, count), BF16),
            jax.ShapeDtypeStruct((count, depth), BF16),
        ],
        scratch_shapes=[pltpu.VMEM((depth, count), BF16), pltpu.SemaphoreType.DMA(())],
        compiler_params=params(56),
        cost_estimate=pl.CostEstimate(
            flops=8 * count * depth, bytes_accessed=20 * MIB, transcendentals=count
        ),
        name="unit_protos",
    )(place, weight)


def swap(value):
    return lax.ppermute(value, "c", [(0, 1), (1, 0)])


def turn(value, by, size):
    return lax.ppermute(value, "z", [(i, (i + by) % size) for i in range(size)])


def copied(value, count):
    return jnp.broadcast_to(value[None], (count,) + value.shape)


def on_device(size, teacher_feats, student_feats, proto_weight):
    depth, held = proto_weight.shape
    devices = size["yl"] * size["x"] * size["c"]
    chips = size["yl"] * size["x"]
    plane = chips * size["yh"]
    pillar = size["z"] * size["c"]
    count = held // devices
    rows = teacher_feats.shape[0]
    core = lax.axis_index("c").reshape(1)
    level = lax.axis_index("z")

    near = exchange(copied(unit_rows(teacher_feats), chips), CHIPS)
    cols, protos = unit_protos(lax.axis_index(DP).reshape(1), proto_weight, count)
    stud_own = unit_rows(student_feats)
    near, protos, cols = lax.optimization_barrier((near, protos, cols))
    far = swap(near)
    stud_own, near = lax.optimization_barrier((stud_own, near))
    stud_near = lax.all_gather(stud_own, CHIPS)

    parts = None
    extra = None
    for step in range(ITERS):
        if step == ITERS - 1:
            extra = totals(core, protos, stud_near, stud_far)
        col, copies = sweep(core, parts, extra, protos, near, far, plane)
        parts = spread(copies, pillar)
        if step == 0:
            stud_near, parts = lax.optimization_barrier((stud_near, parts))
            stud_far = swap(stud_near)

    diff, mine_feat, other_feat = differences(
        core, parts, col, protos, cols, near, far, stud_near, stud_far
    )
    given_feat = swap(other_feat)
    own, *others = cuts(level.reshape(1), mine_feat, given_feat, size["z"])
    turned = [turn(part, by + 1, size["z"]) for by, part in enumerate(others)]
    codes = exchange(proto_part(diff, stud_near, stud_far, devices), DP)
    *turned, codes = lax.optimization_barrier((*turned, codes))
    proto_grad = decoded(codes)
    feat = joined(own, turned).reshape(plane, -1, rows)
    feat = jnp.sum(exchange(feat, PLANE), axis=0)
    feat = exchange(copied(feat, size["z"] * size["yh"]), PROTO)
    feature_grad = 512.0 * feat.reshape(depth, rows).T
    return feature_grad, proto_grad


def solution(mesh):
    split = jax.sharding.Mesh(mesh.devices.reshape(2, 4, 2, 4, 2), AXES)
    return jax.shard_map(
        functools.partial(on_device, dict(split.shape)),
        mesh=split,
        in_specs=(P(DP, None), P(DP, None), P(None, PROTO)),
        out_specs=(P(DP, None), P(DP, PROTO)),
        check_vma=False,
    )
```

profile of v0, /device:TPU:0, one launch (start us, length us, event | category | flops | bytes accessed | tf_op | source)
XLA Modules:
  0.0 243.4 jit_solution(549841186891680229)
XLA Ops:
  7.2 1.0 fusion.2
  8.2 1.0 fusion.3
  9.2 1.0 broadcast_in_dim.4
  10.3 5.4 %all-to-all-start = ((bf16[8,256,256]{2,1,0:T(8,128)(2,1)}), bf16[8,256,256]{2,1,0:T(8,128)(2,1)S(1)}, u32[]{:S(2)}, u32[]{:S(2)}) async-start(bf16[8,256,256]{2,1,0:T(8,128)(2,1)} %broadcast_in_dim.4), calls=%async_computation | async-start | bytes 2097152 | tf_op jit(solution)/shard_map/all_to_all | solution.py:206
  15.7 3.0 %unit_protos.1 = (bf16[256,2048]{1,0:T(8,128)(2,1)}, bf16[2048,256]{1,0:T(8,128)(2,1)}) custom-call(s32[1]{0:T(128)} %bitcast.2.place_ref, bf16[256,32768]{1,0:T(8,128)(2,1)} %weight_ref.1), custom_call_target="tpu_custom_call" | custom-call | flops 4194304 | bytes 20971520 | tf_op jit(solution)/shard_map/unit_protos/pallas_call | solution.py:467
  19.6 11.7 %all-to-all-done.refs_2_.refs_3_.refs_4_.near_ref = bf16[8,256,256]{2,1,0:T(8,128)(2,1)S(1)} async-done(((bf16[8,256,256]{2,1,0:T(8,128)(2,1)}), bf16[8,256,256]{2,1,0:T(8,128)(2,1)S(1)}, u32[]{:S(2)}, u32[]{:S(2)}) %all-to-all-start) | async-done | bytes 1048608 | tf_op jit(solution)/shard_map/all_to_all | solution.py:206
  31.5 2.6 %collective-permute-done.refs_3_.refs_4_.refs_5_.far_ref = bf16[8,256,256]{2,1,0:T(8,128)(2,1)S(1)} collective-permute-done((bf16[8,256,256]{2,1,0:T(8,128)(2,1)S(1)}, bf16[8,256,256]{2,1,0:T(8,128)(2,1)S(1)}, u32[]{:S(2)}, u32[]{:S(2)}) %collective-permute-start) | collective-permute-done | bytes 1048608 | tf_op jit(solution)/shard_map/ppermute | solution.py:485
  34.1 1.2 copy-done
  35.3 9.6 %sweep.3 = (f32[2048,128]{1,0:T(8,128)}, f32[16,32,128]{2,1,0:T(8,128)S(1)}) custom-call(s32[1]{0:T(128)} %bitcast.1.refs_0_.core_ref, bf16[2048,256]{1,0:T(8,128)(2,1)S(1)} %copy-done, bf16[8,256,256]{2,1,0:T(8,128)(2,1)S(1)} %all-to-all-done.refs_2_.refs_3_.refs_4_.near_ref, bf16[8,256,256]{2,1,0:T(8,128)(2,1)S(1)} %collective-permute-done.refs_3_.refs_4_.refs_5_.far_ref), custom_call_target="tpu_custom_call" | custom-call | tf_op jit(solution)/shard_map/sweep/pallas_call | solution.py:129
  44.9 15.1 %all_to_all.50.in_ref = f32[16,32,128]{2,1,0:T(8,128)S(1)} all-to-all(f32[16,32,128]{2,1,0:T(8,128)S(1)} %get-tuple-element.32), channel_id=1, replica_groups=mesh['yl'=2,'x'=4,'c'=2,'z'=4,'yh'=2] {'yl','x','yh'}, dimensions={0} | all-to-all | bytes 524288 | tf_op jit(solution)/shard_map/all_to_all | solution.py:206
  60.0 11.5 %all_to_all.51.refs_1_ = f32[8,32,128]{2,1,0:T(8,128)S(1)} all-to-all(f32[8,32,128]{2,1,0:T(8,128)S(1)} %hop.3), channel_id=1, replica_groups=mesh['yl'=2,'x'=4,'c'=2,'z'=4,'yh'=2] {'z','c'}, dimensions={0} | all-to-all | bytes 262144 | tf_op jit(solution)/shard_map/all_to_all | solution.py:206
  71.5 9.9 %sweep.4 = (f32[2048,128]{1,0:T(8,128)}, f32[16,32,128]{2,1,0:T(8,128)S(1)}) custom-call(s32[1]{0:T(128)} %bitcast.1.refs_0_.core_ref, f32[8,32,128]{2,1,0:T(8,128)S(1)} %all_to_all.51.refs_1_, bf16[2048,256]{1,0:T(8,128)(2,1)S(1)} %copy-done.1, bf16[8,256,256]{2,1,0:T(8,128)(2,1)S(1)} %all-to-all-done.refs_2_.refs_3_.refs_4_.near_ref, ...), custom_call_target="tpu_custom_call" | custom-call | tf_op jit(solution)/shard_map/sweep/pallas_call | solution.py:129
  81.4 13.3 %all_to_all.52.in_ref = f32[16,32,128]{2,1,0:T(8,128)S(1)} all-to-all(f32[16,32,128]{2,1,0:T(8,128)S(1)} %get-tuple-element.34), channel_id=1, replica_groups=mesh['yl'=2,'x'=4,'c'=2,'z'=4,'yh'=2] {'yl','x','yh'}, dimensions={0} | all-to-all | bytes 524288 | tf_op jit(solution)/shard_map/all_to_all | solution.py:206
  95.3 4.4 %all-to-all-start.4 = ((f32[8,32,128]{2,1,0:T(8,128)}), f32[8,32,128]{2,1,0:T(8,128)S(1)}, u32[]{:S(2)}, u32[]{:S(2)}) async-start(f32[8,32,128]{2,1,0:T(8,128)} %hop.4), calls=%async_computation.4 | async-start | bytes 262144 | tf_op jit(solution)/shard_map/all_to_all | solution.py:206
  99.8 1.2 copy-done.2
  101.0 6.4 %totals.1.refs_2_ = f32[32,128]{1,0:T(8,128)S(1)} custom-call(s32[1]{0:T(128)} %bitcast.1.refs_0_.core_ref, bf16[2048,256]{1,0:T(8,128)(2,1)S(1)} %copy-done.1, bf16[8,256,256]{2,1,0:T(8,128)(2,1)S(1)} %bitcast.10, bf16[8,256,256]{2,1,0:T(8,128)(2,1)} %collective-permute-done.1.far_ref.stud_far_ref), custom_call_target="tpu_custom_call" | custom-call | flops 4294967296 | bytes 4194304 | tf_op jit(solution)/shard_map/totals/pallas_call | solution.py:172
  107.4 9.2 %sweep.5 = (f32[2048,128]{1,0:T(8,128)S(1)}, f32[16,64,128]{2,1,0:T(8,128)S(1)}) custom-call(s32[1]{0:T(128)} %bitcast.1.refs_0_.core_ref, f32[8,32,128]{2,1,0:T(8,128)S(1)} %all-to-all-done.4.refs_1_, f32[32,128]{1,0:T(8,128)S(1)} %totals.1.refs_2_, bf16[2048,256]{1,0:T(8,128)(2,1)S(1)} %copy-done.1, ...), custom_call_target="tpu_custom_call" | custom-call | tf_op jit(solution)/shard_map/sweep/pallas_call | solution.py:129
  116.6 15.4 %all_to_all.53.in_ref = f32[16,64,128]{2,1,0:T(8,128)S(1)} all-to-all(f32[16,64,128]{2,1,0:T(8,128)S(1)} %get-tuple-element.36), channel_id=1, replica_groups=mesh['yl'=2,'x'=4,'c'=2,'z'=4,'yh'=2] {'yl','x','yh'}, dimensions={0} | all-to-all | bytes 1048576 | tf_op jit(solution)/shard_map/all_to_all | solution.py:206
  132.0 11.6 %all_to_all.54.parts_ref = f32[8,64,128]{2,1,0:T(8,128)S(1)} all-to-all(f32[8,64,128]{2,1,0:T(8,128)S(1)} %hop.5), channel_id=1, replica_groups=mesh['yl'=2,'x'=4,'c'=2,'z'=4,'yh'=2] {'z','c'}, dimensions={0} | all-to-all | bytes 524288 | tf_op jit(solution)/shard_map/all_to_all | solution.py:206
  143.7 21.5 %differences.1 = (bf16[2048,4096]{1,0:T(8,128)(2,1)}, f32[8,256,256]{2,1,0:T(8,128)S(1)}, f32[8,256,256]{2,1,0:T(8,128)}) custom-call(s32[1]{0:T(128)} %bitcast.1.refs_0_.core_ref, f32[8,64,128]{2,1,0:T(8,128)S(1)} %all_to_all.54.parts_ref, f32[2048,128]{1,0:T(8,128)S(1)} %get-tuple-element.37.col_ref, bf16[2048,256]{1,0:T(8,128)(2,1)S(1)} %copy-done.1, ...), custom_call_target="tpu_custom_call" | custom-call | tf_op jit(solution)/shard_map/differences/pallas_call | solution.py:270
  165.2 1.3 copy-done.4
  166.5 10.8 %proto_part.1 = bf16[16,16,2176]{2,1,0:T(8,128)(2,1)} custom-call(bf16[2048,4096]{1,0:T(8,128)(2,1)} %get-tuple-element.45.diff_ref, bf16[8,256,256]{2,1,0:T(8,128)(2,1)} %bitcast.9, bf16[8,256,256]{2,1,0:T(8,128)(2,1)} %collective-permute-done.1.far_ref.stud_far_ref), custom_call_target="tpu_custom_call" | custom-call | flops 4294967296 | bytes 20971520 | tf_op jit(solution)/shard_map/proto_part/pallas_call | solution.py:376
  177.3 3.8 %all-to-all-start.7 = ((bf16[16,16,2176]{2,1,0:T(8,128)(2,1)}), bf16[16,16,2176]{2,1,0:T(8,128)(2,1)S(1)}, u32[]{:S(2)}, u32[]{:S(2)}) async-start(bf16[16,16,2176]{2,1,0:T(8,128)(2,1)} %proto_part.1), calls=%async_computation.7 | async-start | bytes 2228224 | tf_op jit(solution)/shard_map/all_to_all | solution.py:206
  181.2 3.0 %cuts.1 = (f32[8,64,256]{2,1,0:T(8,128)S(1)}, bf16[8,80,256]{2,1,0:T(8,128)(2,1)}, bf16[8,80,256]{2,1,0:T(8,128)(2,1)}, bf16[8,80,256]{2,1,0:T(8,128)(2,1)S(1)}) custom-call(s32[1]{0:T(128)} %bitcast.level_ref, f32[8,256,256]{2,1,0:T(8,128)S(1)} %copy-done.5, f32[8,256,256]{2,1,0:T(8,128)} %collective-permute-done.2.given_ref), custom_call_target="tpu_custom_call" | custom-call | tf_op jit(solution)/shard_map/cuts/pallas_call | solution.py:416
  185.5 2.1 collective-permute-start.4
  188.2 10.1 %all-to-all-done.7.code_ref = bf16[16,16,2176]{2,1,0:T(8,128)(2,1)S(1)} async-done(((bf16[16,16,2176]{2,1,0:T(8,128)(2,1)}), bf16[16,16,2176]{2,1,0:T(8,128)(2,1)S(1)}, u32[]{:S(2)}, u32[]{:S(2)}) %all-to-all-start.7) | async-done | bytes 1114144 | tf_op jit(solution)/shard_map/all_to_all | solution.py:206
  198.3 5.1 %collective-permute-done.3.refs_0_ = bf16[8,80,256]{2,1,0:T(8,128)(2,1)S(1)} collective-permute-done((bf16[8,80,256]{2,1,0:T(8,128)(2,1)}, bf16[8,80,256]{2,1,0:T(8,128)(2,1)S(1)}, u32[]{:S(2)}, u32[]{:S(2)}) %collective-permute-start.3) | collective-permute-done | bytes 327712 | tf_op jit(solution)/shard_map/ppermute | solution.py:489
  204.1 1.0 copy-done.8
  205.6 15.9 %all_to_all.55 = f32[16,32,256]{2,1,0:T(8,128)S(1)} all-to-all(f32[16,32,256]{2,1,0:T(8,128)S(1)} %bitcast.12), channel_id=1, replica_groups=mesh['yl'=2,'x'=4,'c'=2,'z'=4,'yh'=2] {'yl','x','yh'}, dimensions={0} | all-to-all | bytes 1048576 | tf_op jit(solution)/shard_map/all_to_all | solution.py:206
  222.3 4.6 %all-to-all-start.9 = ((f32[8,32,256]{2,1,0:T(8,128)}), f32[8,32,256]{2,1,0:T(8,128)S(1)}, u32[]{:S(2)}, u32[]{:S(2)}) async-start(f32[8,32,256]{2,1,0:T(8,128)} %broadcast_in_dim.5), calls=%async_computation.9 | async-start | bytes 524288 | tf_op jit(solution)/shard_map/all_to_all | solution.py:206
  226.9 2.1 decoded.1
  229.0 6.7 %all-to-all-done.9 = f32[8,32,256]{2,1,0:T(8,128)S(1)} async-done(((f32[8,32,256]{2,1,0:T(8,128)}), f32[8,32,256]{2,1,0:T(8,128)S(1)}, u32[]{:S(2)}, u32[]{:S(2)}) %all-to-all-start.9) | async-done | bytes 262176 | tf_op jit(solution)/shard_map/all_to_all | solution.py:206
  (41 shorter events, 6.5 us)
Async XLA Ops:
  10.3 21.1 %all-to-all-start = ((bf16[8,256,256]{2,1,0:T(8,128)(2,1)}), bf16[8,256,256]{2,1,0:T(8,128)(2,1)S(1)}, u32[]{:S(2)}, u32[]{:S(2)}) async-start(bf16[8,256,256]{2,1,0:T(8,128)(2,1)} %broadcast_in_dim.4), calls=%async_computation | async-start | bytes 2097152 | tf_op jit(solution)/shard_map/all_to_all | solution.py:206
  15.6 55.8 %all-gather.3.cloned.1.call-start = ((), (), s32[]{:S(2)}) async-start(), calls=%async_computation.10 | async-start | bytes 1179648 | tf_op jit(solution)/shard_map/all_gather | solution.py:513
  15.7 3.0 %copy-start.9 = (bf16[256,256]{1,0:T(8,128)(2,1)S(1)}, bf16[256,256]{1,0:T(8,128)(2,1)}, u32[]{:S(2)}) copy-start(bf16[256,256]{1,0:T(8,128)(2,1)} %param.4) | copy-start | bytes 393220
  31.4 2.7 %collective-permute-start = (bf16[8,256,256]{2,1,0:T(8,128)(2,1)S(1)}, bf16[8,256,256]{2,1,0:T(8,128)(2,1)S(1)}, u32[]{:S(2)}, u32[]{:S(2)}) collective-permute-start(bf16[8,256,256]{2,1,0:T(8,128)(2,1)S(1)} %all-to-all-done.refs_2_.refs_3_.refs_4_.near_ref), channel_id=1, source_target_pairs={{0,8},{8,0},{1,9},{9,1},{2,10},{10,2},{3,11},{11,3},{4,12},{12,4},... | collective-permute-start | bytes 3145736 | tf_op jit(solution)/shard_map/ppermute | solution.py:485
  34.1 1.2 copy-start
  35.3 36.1 %copy-start.1 = (bf16[2048,256]{1,0:T(8,128)(2,1)S(1)}, bf16[2048,256]{1,0:T(8,128)(2,1)}, u32[]{:S(2)}) copy-start(bf16[2048,256]{1,0:T(8,128)(2,1)} %get-tuple-element.30.refs_1_.refs_2_.protos_ref.refs_3_) | copy-start | bytes 3145732
  71.5 28.3 %collective-permute-start.1 = (bf16[8,256,256]{2,1,0:T(8,128)(2,1)}, bf16[8,256,256]{2,1,0:T(8,128)(2,1)}, u32[]{:S(2)}, u32[]{:S(2)}) collective-permute-start(bf16[8,256,256]{2,1,0:T(8,128)(2,1)} %bitcast.8), channel_id=1, source_target_pairs={{0,8},{8,0},{1,9},{9,1},{2,10},{10,2},{3,11},{11,3},{4,12},{12,4},... | collective-permute-start | bytes 3145736 | tf_op jit(solution)/shard_map/ppermute | solution.py:485
  95.3 12.0 %all-to-all-start.4 = ((f32[8,32,128]{2,1,0:T(8,128)}), f32[8,32,128]{2,1,0:T(8,128)S(1)}, u32[]{:S(2)}, u32[]{:S(2)}) async-start(f32[8,32,128]{2,1,0:T(8,128)} %hop.4), calls=%async_computation.4 | async-start | bytes 262144 | tf_op jit(solution)/shard_map/all_to_all | solution.py:206
  99.7 1.2 copy-start.2
  107.4 36.3 %copy-start.3 = (bf16[2048,256]{1,0:T(8,128)(2,1)S(1)}, bf16[2048,256]{1,0:T(8,128)(2,1)}, u32[]{:S(2)}) copy-start(bf16[2048,256]{1,0:T(8,128)(2,1)} %all-gather.3.cloned.1.call-done) | copy-start | bytes 3145732
  107.4 36.3 %copy-start.6 = (bf16[256,2048]{1,0:T(8,128)(2,1)S(1)}, bf16[256,2048]{1,0:T(8,128)(2,1)}, u32[]{:S(2)}) copy-start(bf16[256,2048]{1,0:T(8,128)(2,1)} %get-tuple-element.38.cols_ref) | copy-start | bytes 3145732
  165.2 1.3 copy-start.4
  166.5 14.7 %collective-permute-start.2 = (f32[8,256,256]{2,1,0:T(8,128)}, f32[8,256,256]{2,1,0:T(8,128)}, u32[]{:S(2)}, u32[]{:S(2)}) collective-permute-start(f32[8,256,256]{2,1,0:T(8,128)} %get-tuple-element.40), channel_id=1, source_target_pairs={{0,8},{8,0},{1,9},{9,1},{2,10},{10,2},{3,11},{11,3},{4,12},{12,4},... | collective-permute-start | bytes 6291464 | tf_op jit(solution)/shard_map/ppermute | solution.py:485
  177.3 3.9 %copy-start.5 = (f32[8,256,256]{2,1,0:T(8,128)S(1)}, f32[8,256,256]{2,1,0:T(8,128)}, u32[]{:S(2)}) copy-start(f32[8,256,256]{2,1,0:T(8,128)} %copy-done.4) | copy-start | bytes 6291460
  177.3 21.0 %all-to-all-start.7 = ((bf16[16,16,2176]{2,1,0:T(8,128)(2,1)}), bf16[16,16,2176]{2,1,0:T(8,128)(2,1)S(1)}, u32[]{:S(2)}, u32[]{:S(2)}) async-start(bf16[16,16,2176]{2,1,0:T(8,128)(2,1)} %proto_part.1), calls=%async_computation.7 | async-start | bytes 2228224 | tf_op jit(solution)/shard_map/all_to_all | solution.py:206
  184.2 0.8 copy-start.7
  185.0 18.5 %collective-permute-start.3 = (bf16[8,80,256]{2,1,0:T(8,128)(2,1)}, bf16[8,80,256]{2,1,0:T(8,128)(2,1)S(1)}, u32[]{:S(2)}, u32[]{:S(2)}) collective-permute-start(bf16[8,80,256]{2,1,0:T(8,128)(2,1)} %get-tuple-element.42), channel_id=1, source_target_pairs={{0,2},{2,4},{4,6},{6,0},{1,3},{3,5},{5,7},{7,1},{8,10},{10,12},{12... | collective-permute-start | bytes 983048 | tf_op jit(solution)/shard_map/ppermute | solution.py:489
  185.5 17.9 %collective-permute-start.4 = (bf16[8,80,256]{2,1,0:T(8,128)(2,1)}, bf16[8,80,256]{2,1,0:T(8,128)(2,1)S(1)}, u32[]{:S(2)}, u32[]{:S(2)}) collective-permute-start(bf16[8,80,256]{2,1,0:T(8,128)(2,1)} %get-tuple-element.43), channel_id=1, source_target_pairs={{0,4},{2,6},{4,0},{6,2},{1,5},{3,7},{5,1},{7,3},{8,12},{10,14},{12... | collective-permute-start | bytes 983048 | tf_op jit(solution)/shard_map/ppermute | solution.py:489
  187.6 16.5 %collective-permute-start.5 = (bf16[8,80,256]{2,1,0:T(8,128)(2,1)S(1)}, bf16[8,80,256]{2,1,0:T(8,128)(2,1)S(1)}, u32[]{:S(2)}, u32[]{:S(2)}) collective-permute-start(bf16[8,80,256]{2,1,0:T(8,128)(2,1)S(1)} %get-tuple-element.44), channel_id=1, source_target_pairs={{0,6},{2,0},{4,2},{6,4},{1,7},{3,1},{5,3},{7,5},{8,14},{10,8},{12,... | collective-permute-start | bytes 983048 | tf_op jit(solution)/shard_map/ppermute | solution.py:489
  204.1 1.0 copy-start.8
  222.3 13.4 %all-to-all-start.9 = ((f32[8,32,256]{2,1,0:T(8,128)}), f32[8,32,256]{2,1,0:T(8,128)S(1)}, u32[]{:S(2)}, u32[]{:S(2)}) async-start(f32[8,32,256]{2,1,0:T(8,128)} %broadcast_in_dim.5), calls=%async_computation.9 | async-start | bytes 524288 | tf_op jit(solution)/shard_map/all_to_all | solution.py:206
Sparse Core Ops, SparseCore 0:
  31.5 39.0 all-gather.2
where the time goes:
time: 244 us; the launch traced here: 243 us
  blocking collectives  82.7 us (34%)
  Pallas kernels  76.8 us (31%)
  waiting for transfers between devices  36.9 us (15%)
  starting transfers between devices  21.6 us (9%)
  between operations  14.2 us (6%)
  local copies, waits for them, and re-layouts  8.21 us (3%)
  other arithmetic  2.96 us (1%)
    all_to_all x6, blocking collectives, exchange(): return lax.all_to_all(parts, axes, 0, 0, tiled=True)  82.7 us
    pallas_call x3, Pallas kernels, sweep(): pl.pallas_call(functools.partial(sweep_kernel, copies, tile, parts is not...  28.7 us
    all_to_all x4, waiting for transfers between devices, exchange(): return lax.all_to_all(parts, axes, 0, 0, tiled=True)  28.5 us
    pallas_call x1, Pallas kernels, differences(): pl.pallas_call(functools.partial(diff_kernel, tile), in_specs=[smem()] +...  21.5 us
    all_to_all x4, starting transfers between devices, exchange(): return lax.all_to_all(parts, axes, 0, 0, tiled=True)  18.2 us
    pallas_call x1, Pallas kernels, proto_part(): pl.pallas_call(functools.partial(pgrad_kernel, tile), in_specs=[pl.BlockS...  10.8 us
    unnamed x21, local copies, waits for them, and re-layouts  6.44 us
    pallas_call x1, Pallas kernels, totals(): pl.pallas_call(functools.partial(totals_kernel, tile), in_specs=[smem()]...  6.39 us
  transfers between devices with their start and end apart: 11, of which 6 were waited for; matrix products, arithmetic and copies ran while one was open for 0% of the time, Pallas kernels for 19%

commit v1 on v0

--- a/solution.py
+++ b/solution.py
@@ -59,6 +59,23 @@
     return pl.BlockSpec(memory_space=pltpu.SMEM)
 
 
+def unit_copies_kernel(feats_ref, out_ref):
+    unit = unit_rows(feats_ref[...])
+    for copy in range(out_ref.shape[0]):
+        out_ref[copy] = unit
+
+
+def unit_copies(feats, copies):
+    return pl.pallas_call(
+        unit_copies_kernel,
+        in_specs=[vmem()],
+        out_specs=vmem(),
+        out_shape=jax.ShapeDtypeStruct((copies,) + feats.shape, BF16),
+        compiler_params=params(8),
+        name="unit_copies",
+    )(feats)
+
+
 def block_of(near_ref, far_ref, block):
     pairs = near_ref.shape[0]
     return near_ref[block] if block < pairs else far_ref[block - pairs]
@@ -504,7 +521,7 @@
     core = lax.axis_index("c").reshape(1)
     level = lax.axis_index("z")
 
-    near = exchange(copied(unit_rows(teacher_feats), chips), CHIPS)
+    near = exchange(unit_copies(teacher_feats, chips), CHIPS)
     cols, protos = unit_protos(lax.axis_index(DP).reshape(1), proto_weight, count)
     stud_own = unit_rows(student_feats)
     near, protos, cols = lax.optimization_barrier((near, protos, cols))

time: 244 us -> 243 us (level)
    unnamed x21 -> x19, local copies, waits for them, and re-layouts: 6.44 us -> 7.1 us
where the time goes in v1:
time: 243 us; the launch traced here: 242 us
  blocking collectives  82.7 us (34%)
  Pallas kernels  77.6 us (32%)
  waiting for transfers between devices  36.9 us (15%)
  starting transfers between devices  21.4 us (9%)
  between operations  14.2 us (6%)
  local copies, waits for them, and re-layouts  7.83 us (3%)
    all_to_all x6, blocking collectives, exchange(): return lax.all_to_all(parts, axes, 0, 0, tiled=True)  82.7 us
    pallas_call x3, Pallas kernels, sweep(): pl.pallas_call(functools.partial(sweep_kernel, copies, tile, parts is not...  28.7 us
    all_to_all x4, waiting for transfers between devices, exchange(): return lax.all_to_all(parts, axes, 0, 0, tiled=True)  28.1 us
    pallas_call x1, Pallas kernels, differences(): pl.pallas_call(functools.partial(diff_kernel, tile), in_specs=[smem()] +...  21.5 us
    all_to_all x4, starting transfers between devices, exchange(): return lax.all_to_all(parts, axes, 0, 0, tiled=True)  18 us
    pallas_call x1, Pallas kernels, proto_part(): pl.pallas_call(functools.partial(pgrad_kernel, tile), in_specs=[pl.BlockS...  10.8 us
    unnamed x19, local copies, waits for them, and re-layouts  7.1 us
    pallas_call x1, Pallas kernels, totals(): pl.pallas_call(functools.partial(totals_kernel, tile), in_specs=[smem()]...  6.4 us
  transfers between devices with their start and end apart: 11, of which 6 were waited for; matrix products, arithmetic and copies ran while one was open for 0% of the time, Pallas kernels for 19%

profile of v1, /device:TPU:0, one launch (start us, length us, event | category | flops | bytes accessed | tf_op | source)
XLA Modules:
  0.0 241.6 jit_solution(3615300469955342576)
XLA Ops:
  7.2 0.9 copy-done.7
  8.1 1.1 unit_copies.1
  9.2 5.4 %all-to-all-start = ((bf16[8,256,256]{2,1,0:T(8,128)(2,1)}), bf16[8,256,256]{2,1,0:T(8,128)(2,1)S(1)}, u32[]{:S(2)}, u32[]{:S(2)}) async-start(bf16[8,256,256]{2,1,0:T(8,128)(2,1)} %unit_copies.1), calls=%async_computation | async-start | bytes 2097152 | tf_op jit(solution)/shard_map/all_to_all | solution.py:223
  14.7 3.0 %unit_protos.1 = (bf16[256,2048]{1,0:T(8,128)(2,1)}, bf16[2048,256]{1,0:T(8,128)(2,1)}) custom-call(s32[1]{0:T(128)} %bitcast.2.place_ref, bf16[256,32768]{1,0:T(8,128)(2,1)} %weight_ref.1), custom_call_target="tpu_custom_call" | custom-call | flops 4194304 | bytes 20971520 | tf_op jit(solution)/shard_map/unit_protos/pallas_call | solution.py:484
  18.6 11.7 %all-to-all-done.refs_2_.refs_3_.refs_4_.near_ref = bf16[8,256,256]{2,1,0:T(8,128)(2,1)S(1)} async-done(((bf16[8,256,256]{2,1,0:T(8,128)(2,1)}), bf16[8,256,256]{2,1,0:T(8,128)(2,1)S(1)}, u32[]{:S(2)}, u32[]{:S(2)}) %all-to-all-start) | async-done | bytes 1048608 | tf_op jit(solution)/shard_map/all_to_all | solution.py:223
  30.4 2.6 %collective-permute-done.refs_3_.refs_4_.refs_5_.far_ref = bf16[8,256,256]{2,1,0:T(8,128)(2,1)S(1)} collective-permute-done((bf16[8,256,256]{2,1,0:T(8,128)(2,1)S(1)}, bf16[8,256,256]{2,1,0:T(8,128)(2,1)S(1)}, u32[]{:S(2)}, u32[]{:S(2)}) %collective-permute-start) | collective-permute-done | bytes 1048608 | tf_op jit(solution)/shard_map/ppermute | solution.py:502
  33.1 1.2 copy-done
  34.3 9.6 %sweep.3 = (f32[2048,128]{1,0:T(8,128)}, f32[16,32,128]{2,1,0:T(8,128)S(1)}) custom-call(s32[1]{0:T(128)} %bitcast.1.refs_0_.core_ref, bf16[2048,256]{1,0:T(8,128)(2,1)S(1)} %copy-done, bf16[8,256,256]{2,1,0:T(8,128)(2,1)S(1)} %all-to-all-done.refs_2_.refs_3_.refs_4_.near_ref, bf16[8,256,256]{2,1,0:T(8,128)(2,1)S(1)} %collective-permute-done.refs_3_.refs_4_.refs_5_.far_ref), custom_call_target="tpu_custom_call" | custom-call | tf_op jit(solution)/shard_map/sweep/pallas_call | solution.py:146
  43.9 15.0 %all_to_all.50.in_ref = f32[16,32,128]{2,1,0:T(8,128)S(1)} all-to-all(f32[16,32,128]{2,1,0:T(8,128)S(1)} %get-tuple-element.32), channel_id=1, replica_groups=mesh['yl'=2,'x'=4,'c'=2,'z'=4,'yh'=2] {'yl','x','yh'}, dimensions={0} | all-to-all | bytes 524288 | tf_op jit(solution)/shard_map/all_to_all | solution.py:223
  58.9 11.4 %all_to_all.51.refs_1_ = f32[8,32,128]{2,1,0:T(8,128)S(1)} all-to-all(f32[8,32,128]{2,1,0:T(8,128)S(1)} %hop.3), channel_id=1, replica_groups=mesh['yl'=2,'x'=4,'c'=2,'z'=4,'yh'=2] {'z','c'}, dimensions={0} | all-to-all | bytes 262144 | tf_op jit(solution)/shard_map/all_to_all | solution.py:223
  70.4 10.0 %sweep.4 = (f32[2048,128]{1,0:T(8,128)}, f32[16,32,128]{2,1,0:T(8,128)S(1)}) custom-call(s32[1]{0:T(128)} %bitcast.1.refs_0_.core_ref, f32[8,32,128]{2,1,0:T(8,128)S(1)} %all_to_all.51.refs_1_, bf16[2048,256]{1,0:T(8,128)(2,1)S(1)} %copy-done.1, bf16[8,256,256]{2,1,0:T(8,128)(2,1)S(1)} %all-to-all-done.refs_2_.refs_3_.refs_4_.near_ref, ...), custom_call_target="tpu_custom_call" | custom-call | tf_op jit(solution)/shard_map/sweep/pallas_call | solution.py:146
  80.4 13.3 %all_to_all.52.in_ref = f32[16,32,128]{2,1,0:T(8,128)S(1)} all-to-all(f32[16,32,128]{2,1,0:T(8,128)S(1)} %get-tuple-element.34), channel_id=1, replica_groups=mesh['yl'=2,'x'=4,'c'=2,'z'=4,'yh'=2] {'yl','x','yh'}, dimensions={0} | all-to-all | bytes 524288 | tf_op jit(solution)/shard_map/all_to_all | solution.py:223
  94.3 4.4 %all-to-all-start.4 = ((f32[8,32,128]{2,1,0:T(8,128)}), f32[8,32,128]{2,1,0:T(8,128)S(1)}, u32[]{:S(2)}, u32[]{:S(2)}) async-start(f32[8,32,128]{2,1,0:T(8,128)} %hop.4), calls=%async_computation.4 | async-start | bytes 262144 | tf_op jit(solution)/shard_map/all_to_all | solution.py:223
  98.7 1.2 copy-done.2
  99.9 6.4 %totals.1.refs_2_ = f32[32,128]{1,0:T(8,128)S(1)} custom-call(s32[1]{0:T(128)} %bitcast.1.refs_0_.core_ref, bf16[2048,256]{1,0:T(8,128)(2,1)S(1)} %copy-done.1, bf16[8,256,256]{2,1,0:T(8,128)(2,1)S(1)} %bitcast.10, bf16[8,256,256]{2,1,0:T(8,128)(2,1)} %collective-permute-done.1.far_ref.stud_far_ref), custom_call_target="tpu_custom_call" | custom-call | flops 4294967296 | bytes 4194304 | tf_op jit(solution)/shard_map/totals/pallas_call | solution.py:189
  106.4 9.2 %sweep.5 = (f32[2048,128]{1,0:T(8,128)S(1)}, f32[16,64,128]{2,1,0:T(8,128)S(1)}) custom-call(s32[1]{0:T(128)} %bitcast.1.refs_0_.core_ref, f32[8,32,128]{2,1,0:T(8,128)S(1)} %all-to-all-done.4.refs_1_, f32[32,128]{1,0:T(8,128)S(1)} %totals.1.refs_2_, bf16[2048,256]{1,0:T(8,128)(2,1)S(1)} %copy-done.1, ...), custom_call_target="tpu_custom_call" | custom-call | tf_op jit(solution)/shard_map/sweep/pallas_call | solution.py:146
  115.6 15.4 %all_to_all.53.in_ref = f32[16,64,128]{2,1,0:T(8,128)S(1)} all-to-all(f32[16,64,128]{2,1,0:T(8,128)S(1)} %get-tuple-element.36), channel_id=1, replica_groups=mesh['yl'=2,'x'=4,'c'=2,'z'=4,'yh'=2] {'yl','x','yh'}, dimensions={0} | all-to-all | bytes 1048576 | tf_op jit(solution)/shard_map/all_to_all | solution.py:223
  131.0 11.6 %all_to_all.54.parts_ref = f32[8,64,128]{2,1,0:T(8,128)S(1)} all-to-all(f32[8,64,128]{2,1,0:T(8,128)S(1)} %hop.5), channel_id=1, replica_groups=mesh['yl'=2,'x'=4,'c'=2,'z'=4,'yh'=2] {'z','c'}, dimensions={0} | all-to-all | bytes 524288 | tf_op jit(solution)/shard_map/all_to_all | solution.py:223
  142.6 21.5 %differences.1 = (bf16[2048,4096]{1,0:T(8,128)(2,1)}, f32[8,256,256]{2,1,0:T(8,128)S(1)}, f32[8,256,256]{2,1,0:T(8,128)}) custom-call(s32[1]{0:T(128)} %bitcast.1.refs_0_.core_ref, f32[8,64,128]{2,1,0:T(8,128)S(1)} %all_to_all.54.parts_ref, f32[2048,128]{1,0:T(8,128)S(1)} %get-tuple-element.37.col_ref, bf16[2048,256]{1,0:T(8,128)(2,1)S(1)} %copy-done.1, ...), custom_call_target="tpu_custom_call" | custom-call | tf_op jit(solution)/shard_map/differences/pallas_call | solution.py:287
  164.2 1.3 copy-done.4
  165.5 10.8 %proto_part.1 = bf16[16,16,2176]{2,1,0:T(8,128)(2,1)} custom-call(bf16[2048,4096]{1,0:T(8,128)(2,1)} %get-tuple-element.45.diff_ref, bf16[8,256,256]{2,1,0:T(8,128)(2,1)} %bitcast.9, bf16[8,256,256]{2,1,0:T(8,128)(2,1)} %collective-permute-done.1.far_ref.stud_far_ref), custom_call_target="tpu_custom_call" | custom-call | flops 4294967296 | bytes 20971520 | tf_op jit(solution)/shard_map/proto_part/pallas_call | solution.py:393
  176.3 3.7 %all-to-all-start.7 = ((bf16[16,16,2176]{2,1,0:T(8,128)(2,1)}), bf16[16,16,2176]{2,1,0:T(8,128)(2,1)S(1)}, u32[]{:S(2)}, u32[]{:S(2)}) async-start(bf16[16,16,2176]{2,1,0:T(8,128)(2,1)} %proto_part.1), calls=%async_computation.7 | async-start | bytes 2228224 | tf_op jit(solution)/shard_map/all_to_all | solution.py:223
  180.0 1.6 copy-done.5
  181.6 2.6 %cuts.1 = (f32[8,64,256]{2,1,0:T(8,128)S(1)}, bf16[8,80,256]{2,1,0:T(8,128)(2,1)S(1)}, bf16[8,80,256]{2,1,0:T(8,128)(2,1)}, bf16[8,80,256]{2,1,0:T(8,128)(2,1)S(1)}) custom-call(s32[1]{0:T(128)} %bitcast.level_ref, f32[8,256,256]{2,1,0:T(8,128)S(1)} %copy-done.5, f32[8,256,256]{2,1,0:T(8,128)} %collective-permute-done.2.given_ref), custom_call_target="tpu_custom_call" | custom-call | tf_op jit(solution)/shard_map/cuts/pallas_call | solution.py:433
  184.8 2.1 collective-permute-start.4
  187.5 9.7 %all-to-all-done.7.code_ref = bf16[16,16,2176]{2,1,0:T(8,128)(2,1)S(1)} async-done(((bf16[16,16,2176]{2,1,0:T(8,128)(2,1)}), bf16[16,16,2176]{2,1,0:T(8,128)(2,1)S(1)}, u32[]{:S(2)}, u32[]{:S(2)}) %all-to-all-start.7) | async-done | bytes 1114144 | tf_op jit(solution)/shard_map/all_to_all | solution.py:223
  197.2 5.3 %collective-permute-done.3.refs_0_ = bf16[8,80,256]{2,1,0:T(8,128)(2,1)S(1)} collective-permute-done((bf16[8,80,256]{2,1,0:T(8,128)(2,1)S(1)}, bf16[8,80,256]{2,1,0:T(8,128)(2,1)S(1)}, u32[]{:S(2)}, u32[]{:S(2)}) %collective-permute-start.3) | collective-permute-done | bytes 327712 | tf_op jit(solution)/shard_map/ppermute | solution.py:506
  203.9 15.9 %all_to_all.55 = f32[16,32,256]{2,1,0:T(8,128)S(1)} all-to-all(f32[16,32,256]{2,1,0:T(8,128)S(1)} %bitcast.12), channel_id=1, replica_groups=mesh['yl'=2,'x'=4,'c'=2,'z'=4,'yh'=2] {'yl','x','yh'}, dimensions={0} | all-to-all | bytes 1048576 | tf_op jit(solution)/shard_map/all_to_all | solution.py:223
  220.5 4.6 %all-to-all-start.9 = ((f32[8,32,256]{2,1,0:T(8,128)}), f32[8,32,256]{2,1,0:T(8,128)S(1)}, u32[]{:S(2)}, u32[]{:S(2)}) async-start(f32[8,32,256]{2,1,0:T(8,128)} %broadcast_in_dim.2), calls=%async_computation.9 | async-start | bytes 524288 | tf_op jit(solution)/shard_map/all_to_all | solution.py:223
  225.1 2.1 decoded.1
  227.2 6.7 %all-to-all-done.9 = f32[8,32,256]{2,1,0:T(8,128)S(1)} async-done(((f32[8,32,256]{2,1,0:T(8,128)}), f32[8,32,256]{2,1,0:T(8,128)S(1)}, u32[]{:S(2)}, u32[]{:S(2)}) %all-to-all-start.9) | async-done | bytes 262176 | tf_op jit(solution)/shard_map/all_to_all | solution.py:223
  233.9 0.8 copy.5
  (36 shorter events, 5.1 us)
Async XLA Ops:
  7.2 0.9 copy-start.7
  9.2 21.1 %all-to-all-start = ((bf16[8,256,256]{2,1,0:T(8,128)(2,1)}), bf16[8,256,256]{2,1,0:T(8,128)(2,1)S(1)}, u32[]{:S(2)}, u32[]{:S(2)}) async-start(bf16[8,256,256]{2,1,0:T(8,128)(2,1)} %unit_copies.1), calls=%async_computation | async-start | bytes 2097152 | tf_op jit(solution)/shard_map/all_to_all | solution.py:223
  14.6 55.8 %all-gather.3.cloned.1.call-start = ((), (), s32[]{:S(2)}) async-start(), calls=%async_computation.10 | async-start | bytes 1179648 | tf_op jit(solution)/shard_map/all_gather | solution.py:530
  14.6 3.0 %copy-start.8 = (bf16[256,256]{1,0:T(8,128)(2,1)S(1)}, bf16[256,256]{1,0:T(8,128)(2,1)}, u32[]{:S(2)}) copy-start(bf16[256,256]{1,0:T(8,128)(2,1)} %param.4) | copy-start | bytes 393220
  30.3 2.7 %collective-permute-start = (bf16[8,256,256]{2,1,0:T(8,128)(2,1)S(1)}, bf16[8,256,256]{2,1,0:T(8,128)(2,1)S(1)}, u32[]{:S(2)}, u32[]{:S(2)}) collective-permute-start(bf16[8,256,256]{2,1,0:T(8,128)(2,1)S(1)} %all-to-all-done.refs_2_.refs_3_.refs_4_.near_ref), channel_id=1, source_target_pairs={{0,8},{8,0},{1,9},{9,1},{2,10},{10,2},{3,11},{11,3},{4,12},{12,4},... | collective-permute-start | bytes 3145736 | tf_op jit(solution)/shard_map/ppermute | solution.py:502
  33.1 1.2 copy-start
  34.3 36.1 %copy-start.1 = (bf16[2048,256]{1,0:T(8,128)(2,1)S(1)}, bf16[2048,256]{1,0:T(8,128)(2,1)}, u32[]{:S(2)}) copy-start(bf16[2048,256]{1,0:T(8,128)(2,1)} %get-tuple-element.30.refs_1_.refs_2_.protos_ref.refs_3_) | copy-start | bytes 3145732
  70.4 28.3 %collective-permute-start.1 = (bf16[8,256,256]{2,1,0:T(8,128)(2,1)}, bf16[8,256,256]{2,1,0:T(8,128)(2,1)}, u32[]{:S(2)}, u32[]{:S(2)}) collective-permute-start(bf16[8,256,256]{2,1,0:T(8,128)(2,1)} %bitcast.8), channel_id=1, source_target_pairs={{0,8},{8,0},{1,9},{9,1},{2,10},{10,2},{3,11},{11,3},{4,12},{12,4},... | collective-permute-start | bytes 3145736 | tf_op jit(solution)/shard_map/ppermute | solution.py:502
  94.3 12.0 %all-to-all-start.4 = ((f32[8,32,128]{2,1,0:T(8,128)}), f32[8,32,128]{2,1,0:T(8,128)S(1)}, u32[]{:S(2)}, u32[]{:S(2)}) async-start(f32[8,32,128]{2,1,0:T(8,128)} %hop.4), calls=%async_computation.4 | async-start | bytes 262144 | tf_op jit(solution)/shard_map/all_to_all | solution.py:223
  98.7 1.2 copy-start.2
  106.4 36.3 %copy-start.3 = (bf16[2048,256]{1,0:T(8,128)(2,1)S(1)}, bf16[2048,256]{1,0:T(8,128)(2,1)}, u32[]{:S(2)}) copy-start(bf16[2048,256]{1,0:T(8,128)(2,1)} %all-gather.3.cloned.1.call-done) | copy-start | bytes 3145732
  106.4 36.3 %copy-start.6 = (bf16[256,2048]{1,0:T(8,128)(2,1)S(1)}, bf16[256,2048]{1,0:T(8,128)(2,1)}, u32[]{:S(2)}) copy-start(bf16[256,2048]{1,0:T(8,128)(2,1)} %get-tuple-element.38.cols_ref) | copy-start | bytes 3145732
  164.2 1.3 copy-start.4
  165.5 14.5 %collective-permute-start.2 = (f32[8,256,256]{2,1,0:T(8,128)}, f32[8,256,256]{2,1,0:T(8,128)}, u32[]{:S(2)}, u32[]{:S(2)}) collective-permute-start(f32[8,256,256]{2,1,0:T(8,128)} %get-tuple-element.40), channel_id=1, source_target_pairs={{0,8},{8,0},{1,9},{9,1},{2,10},{10,2},{3,11},{11,3},{4,12},{12,4},... | collective-permute-start | bytes 6291464 | tf_op jit(solution)/shard_map/ppermute | solution.py:502
  176.3 20.9 %all-to-all-start.7 = ((bf16[16,16,2176]{2,1,0:T(8,128)(2,1)}), bf16[16,16,2176]{2,1,0:T(8,128)(2,1)S(1)}, u32[]{:S(2)}, u32[]{:S(2)}) async-start(bf16[16,16,2176]{2,1,0:T(8,128)(2,1)} %proto_part.1), calls=%async_computation.7 | async-start | bytes 2228224 | tf_op jit(solution)/shard_map/all_to_all | solution.py:223
  180.0 1.6 copy-start.5
  184.2 18.3 %collective-permute-start.3 = (bf16[8,80,256]{2,1,0:T(8,128)(2,1)S(1)}, bf16[8,80,256]{2,1,0:T(8,128)(2,1)S(1)}, u32[]{:S(2)}, u32[]{:S(2)}) collective-permute-start(bf16[8,80,256]{2,1,0:T(8,128)(2,1)S(1)} %get-tuple-element.42), channel_id=1, source_target_pairs={{0,2},{2,4},{4,6},{6,0},{1,3},{3,5},{5,7},{7,1},{8,10},{10,12},{12... | collective-permute-start | bytes 983048 | tf_op jit(solution)/shard_map/ppermute | solution.py:506
  184.8 17.7 %collective-permute-start.4 = (bf16[8,80,256]{2,1,0:T(8,128)(2,1)}, bf16[8,80,256]{2,1,0:T(8,128)(2,1)S(1)}, u32[]{:S(2)}, u32[]{:S(2)}) collective-permute-start(bf16[8,80,256]{2,1,0:T(8,128)(2,1)} %get-tuple-element.43), channel_id=1, source_target_pairs={{0,4},{2,6},{4,0},{6,2},{1,5},{3,7},{5,1},{7,3},{8,12},{10,14},{12... | collective-permute-start | bytes 983048 | tf_op jit(solution)/shard_map/ppermute | solution.py:506
  186.9 16.5 %collective-permute-start.5 = (bf16[8,80,256]{2,1,0:T(8,128)(2,1)S(1)}, bf16[8,80,256]{2,1,0:T(8,128)(2,1)S(1)}, u32[]{:S(2)}, u32[]{:S(2)}) collective-permute-start(bf16[8,80,256]{2,1,0:T(8,128)(2,1)S(1)} %get-tuple-element.44), channel_id=1, source_target_pairs={{0,6},{2,0},{4,2},{6,4},{1,7},{3,1},{5,3},{7,5},{8,14},{10,8},{12,... | collective-permute-start | bytes 983048 | tf_op jit(solution)/shard_map/ppermute | solution.py:506
  220.5 13.4 %all-to-all-start.9 = ((f32[8,32,256]{2,1,0:T(8,128)}), f32[8,32,256]{2,1,0:T(8,128)S(1)}, u32[]{:S(2)}, u32[]{:S(2)}) async-start(f32[8,32,256]{2,1,0:T(8,128)} %broadcast_in_dim.2), calls=%async_computation.9 | async-start | bytes 524288 | tf_op jit(solution)/shard_map/all_to_all | solution.py:223
Sparse Core Ops, SparseCore 0:
  30.4 39.0 all-gather.2

commit v2 on v1

--- a/solution.py
+++ b/solution.py
@@ -136,7 +136,7 @@
             out_ref[copy, groups:, :] = extra
 
 
-def sweep(core, parts, extra, protos, near, far, copies, tile=256):
+def sweep(core, parts, extra, protos, near, far, copies, tile=512):
     count = protos.shape[0]
     pairs, rows, _ = near.shape
     total = 2 * pairs * rows

time: 243 us -> 241 us (level)
  transfers between devices with their start and end apart: 11 -> 11, of which waited for: 6 -> 6; matrix products, arithmetic and copies ran while one was open for 0% -> 0% of each run, Pallas kernels for 19% -> 18%
where the time goes in v2:
time: 241 us; the launch traced here: 240 us
  blocking collectives  83.7 us (35%)
  Pallas kernels  75.2 us (31%)
  waiting for transfers between devices  36.9 us (15%)
  starting transfers between devices  21.2 us (9%)
  between operations  14.2 us (6%)
  local copies, waits for them, and re-layouts  7.83 us (3%)
    all_to_all x6, blocking collectives, exchange(): return lax.all_to_all(parts, axes, 0, 0, tiled=True)  83.7 us
    all_to_all x4, waiting for transfers between devices, exchange(): return lax.all_to_all(parts, axes, 0, 0, tiled=True)  28.1 us
    pallas_call x3, Pallas kernels, sweep(): pl.pallas_call(functools.partial(sweep_kernel, copies, tile, parts is not...  26.3 us
    pallas_call x1, Pallas kernels, differences(): pl.pallas_call(functools.partial(diff_kernel, tile), in_specs=[smem()] +...  21.5 us
    all_to_all x4, starting transfers between devices, exchange(): return lax.all_to_all(parts, axes, 0, 0, tiled=True)  17.9 us
    pallas_call x1, Pallas kernels, proto_part(): pl.pallas_call(functools.partial(pgrad_kernel, tile), in_specs=[pl.BlockS...  10.8 us
    unnamed x19, local copies, waits for them, and re-layouts  7.1 us
    pallas_call x1, Pallas kernels, totals(): pl.pallas_call(functools.partial(totals_kernel, tile), in_specs=[smem()]...  6.4 us
  transfers between devices with their start and end apart: 11, of which 6 were waited for; matrix products, arithmetic and copies ran while one was open for 0% of the time, Pallas kernels for 18%

profile of v2, /device:TPU:0, one launch (start us, length us, event | category | flops | bytes accessed | tf_op | source)
XLA Modules:
  0.0 240.0 jit_solution(15966966702718021104)
XLA Ops:
  7.2 0.9 copy-done.7
  8.1 1.1 unit_copies.1
  9.2 5.4 %all-to-all-start = ((bf16[8,256,256]{2,1,0:T(8,128)(2,1)}), bf16[8,256,256]{2,1,0:T(8,128)(2,1)S(1)}, u32[]{:S(2)}, u32[]{:S(2)}) async-start(bf16[8,256,256]{2,1,0:T(8,128)(2,1)} %unit_copies.1), calls=%async_computation | async-start | bytes 2097152 | tf_op jit(solution)/shard_map/all_to_all | solution.py:223
  14.7 3.0 %unit_protos.1 = (bf16[256,2048]{1,0:T(8,128)(2,1)}, bf16[2048,256]{1,0:T(8,128)(2,1)}) custom-call(s32[1]{0:T(128)} %bitcast.2.place_ref, bf16[256,32768]{1,0:T(8,128)(2,1)} %weight_ref.1), custom_call_target="tpu_custom_call" | custom-call | flops 4194304 | bytes 20971520 | tf_op jit(solution)/shard_map/unit_protos/pallas_call | solution.py:484
  18.6 11.7 %all-to-all-done.refs_2_.refs_3_.refs_4_.near_ref = bf16[8,256,256]{2,1,0:T(8,128)(2,1)S(1)} async-done(((bf16[8,256,256]{2,1,0:T(8,128)(2,1)}), bf16[8,256,256]{2,1,0:T(8,128)(2,1)S(1)}, u32[]{:S(2)}, u32[]{:S(2)}) %all-to-all-start) | async-done | bytes 1048608 | tf_op jit(solution)/shard_map/all_to_all | solution.py:223
  30.4 2.6 %collective-permute-done.refs_3_.refs_4_.refs_5_.far_ref = bf16[8,256,256]{2,1,0:T(8,128)(2,1)S(1)} collective-permute-done((bf16[8,256,256]{2,1,0:T(8,128)(2,1)S(1)}, bf16[8,256,256]{2,1,0:T(8,128)(2,1)S(1)}, u32[]{:S(2)}, u32[]{:S(2)}) %collective-permute-start) | collective-permute-done | bytes 1048608 | tf_op jit(solution)/shard_map/ppermute | solution.py:502
  33.1 1.2 copy-done
  34.3 8.8 %sweep.3 = (f32[2048,128]{1,0:T(8,128)}, f32[16,32,128]{2,1,0:T(8,128)S(1)}) custom-call(s32[1]{0:T(128)} %bitcast.1.refs_0_.core_ref, bf16[2048,256]{1,0:T(8,128)(2,1)S(1)} %copy-done, bf16[8,256,256]{2,1,0:T(8,128)(2,1)S(1)} %all-to-all-done.refs_2_.refs_3_.refs_4_.near_ref, bf16[8,256,256]{2,1,0:T(8,128)(2,1)S(1)} %collective-permute-done.refs_3_.refs_4_.refs_5_.far_ref), custom_call_target="tpu_custom_call" | custom-call | tf_op jit(solution)/shard_map/sweep/pallas_call | solution.py:146
  43.1 14.8 %all_to_all.50.in_ref = f32[16,32,128]{2,1,0:T(8,128)S(1)} all-to-all(f32[16,32,128]{2,1,0:T(8,128)S(1)} %get-tuple-element.32), channel_id=1, replica_groups=mesh['yl'=2,'x'=4,'c'=2,'z'=4,'yh'=2] {'yl','x','yh'}, dimensions={0} | all-to-all | bytes 524288 | tf_op jit(solution)/shard_map/all_to_all | solution.py:223
  57.9 11.5 %all_to_all.51.refs_1_ = f32[8,32,128]{2,1,0:T(8,128)S(1)} all-to-all(f32[8,32,128]{2,1,0:T(8,128)S(1)} %hop.3), channel_id=1, replica_groups=mesh['yl'=2,'x'=4,'c'=2,'z'=4,'yh'=2] {'z','c'}, dimensions={0} | all-to-all | bytes 262144 | tf_op jit(solution)/shard_map/all_to_all | solution.py:223
  69.4 9.1 %sweep.4 = (f32[2048,128]{1,0:T(8,128)}, f32[16,32,128]{2,1,0:T(8,128)S(1)}) custom-call(s32[1]{0:T(128)} %bitcast.1.refs_0_.core_ref, f32[8,32,128]{2,1,0:T(8,128)S(1)} %all_to_all.51.refs_1_, bf16[2048,256]{1,0:T(8,128)(2,1)S(1)} %copy-done.1, bf16[8,256,256]{2,1,0:T(8,128)(2,1)S(1)} %all-to-all-done.refs_2_.refs_3_.refs_4_.near_ref, ...), custom_call_target="tpu_custom_call" | custom-call | tf_op jit(solution)/shard_map/sweep/pallas_call | solution.py:146
  78.5 14.5 %all_to_all.52.in_ref = f32[16,32,128]{2,1,0:T(8,128)S(1)} all-to-all(f32[16,32,128]{2,1,0:T(8,128)S(1)} %get-tuple-element.34), channel_id=1, replica_groups=mesh['yl'=2,'x'=4,'c'=2,'z'=4,'yh'=2] {'yl','x','yh'}, dimensions={0} | all-to-all | bytes 524288 | tf_op jit(solution)/shard_map/all_to_all | solution.py:223
  93.7 4.2 %all-to-all-start.4 = ((f32[8,32,128]{2,1,0:T(8,128)}), f32[8,32,128]{2,1,0:T(8,128)S(1)}, u32[]{:S(2)}, u32[]{:S(2)}) async-start(f32[8,32,128]{2,1,0:T(8,128)} %hop.4), calls=%async_computation.4 | async-start | bytes 262144 | tf_op jit(solution)/shard_map/all_to_all | solution.py:223
  97.9 1.2 copy-done.2
  99.1 6.4 %totals.1.refs_2_ = f32[32,128]{1,0:T(8,128)S(1)} custom-call(s32[1]{0:T(128)} %bitcast.1.refs_0_.core_ref, bf16[2048,256]{1,0:T(8,128)(2,1)S(1)} %copy-done.1, bf16[8,256,256]{2,1,0:T(8,128)(2,1)S(1)} %bitcast.10, bf16[8,256,256]{2,1,0:T(8,128)(2,1)} %collective-permute-done.1.far_ref.stud_far_ref), custom_call_target="tpu_custom_call" | custom-call | flops 4294967296 | bytes 4194304 | tf_op jit(solution)/shard_map/totals/pallas_call | solution.py:189
  105.6 8.4 %sweep.5 = (f32[2048,128]{1,0:T(8,128)S(1)}, f32[16,64,128]{2,1,0:T(8,128)S(1)}) custom-call(s32[1]{0:T(128)} %bitcast.1.refs_0_.core_ref, f32[8,32,128]{2,1,0:T(8,128)S(1)} %all-to-all-done.4.refs_1_, f32[32,128]{1,0:T(8,128)S(1)} %totals.1.refs_2_, bf16[2048,256]{1,0:T(8,128)(2,1)S(1)} %copy-done.1, ...), custom_call_target="tpu_custom_call" | custom-call | tf_op jit(solution)/shard_map/sweep/pallas_call | solution.py:146
  114.0 15.4 %all_to_all.53.in_ref = f32[16,64,128]{2,1,0:T(8,128)S(1)} all-to-all(f32[16,64,128]{2,1,0:T(8,128)S(1)} %get-tuple-element.36), channel_id=1, replica_groups=mesh['yl'=2,'x'=4,'c'=2,'z'=4,'yh'=2] {'yl','x','yh'}, dimensions={0} | all-to-all | bytes 1048576 | tf_op jit(solution)/shard_map/all_to_all | solution.py:223
  129.4 11.6 %all_to_all.54.parts_ref = f32[8,64,128]{2,1,0:T(8,128)S(1)} all-to-all(f32[8,64,128]{2,1,0:T(8,128)S(1)} %hop.5), channel_id=1, replica_groups=mesh['yl'=2,'x'=4,'c'=2,'z'=4,'yh'=2] {'z','c'}, dimensions={0} | all-to-all | bytes 524288 | tf_op jit(solution)/shard_map/all_to_all | solution.py:223
  141.0 21.5 %differences.1 = (bf16[2048,4096]{1,0:T(8,128)(2,1)}, f32[8,256,256]{2,1,0:T(8,128)S(1)}, f32[8,256,256]{2,1,0:T(8,128)}) custom-call(s32[1]{0:T(128)} %bitcast.1.refs_0_.core_ref, f32[8,64,128]{2,1,0:T(8,128)S(1)} %all_to_all.54.parts_ref, f32[2048,128]{1,0:T(8,128)S(1)} %get-tuple-element.37.col_ref, bf16[2048,256]{1,0:T(8,128)(2,1)S(1)} %copy-done.1, ...), custom_call_target="tpu_custom_call" | custom-call | tf_op jit(solution)/shard_map/differences/pallas_call | solution.py:287
  162.6 1.3 copy-done.4
  163.9 10.8 %proto_part.1 = bf16[16,16,2176]{2,1,0:T(8,128)(2,1)} custom-call(bf16[2048,4096]{1,0:T(8,128)(2,1)} %get-tuple-element.45.diff_ref, bf16[8,256,256]{2,1,0:T(8,128)(2,1)} %bitcast.9, bf16[8,256,256]{2,1,0:T(8,128)(2,1)} %collective-permute-done.1.far_ref.stud_far_ref), custom_call_target="tpu_custom_call" | custom-call | flops 4294967296 | bytes 20971520 | tf_op jit(solution)/shard_map/proto_part/pallas_call | solution.py:393
  174.7 3.7 %all-to-all-start.7 = ((bf16[16,16,2176]{2,1,0:T(8,128)(2,1)}), bf16[16,16,2176]{2,1,0:T(8,128)(2,1)S(1)}, u32[]{:S(2)}, u32[]{:S(2)}) async-start(bf16[16,16,2176]{2,1,0:T(8,128)(2,1)} %proto_part.1), calls=%async_computation.7 | async-start | bytes 2228224 | tf_op jit(solution)/shard_map/all_to_all | solution.py:223
  178.4 1.6 copy-done.5
  180.0 2.6 %cuts.1 = (f32[8,64,256]{2,1,0:T(8,128)S(1)}, bf16[8,80,256]{2,1,0:T(8,128)(2,1)S(1)}, bf16[8,80,256]{2,1,0:T(8,128)(2,1)}, bf16[8,80,256]{2,1,0:T(8,128)(2,1)S(1)}) custom-call(s32[1]{0:T(128)} %bitcast.level_ref, f32[8,256,256]{2,1,0:T(8,128)S(1)} %copy-done.5, f32[8,256,256]{2,1,0:T(8,128)} %collective-permute-done.2.given_ref), custom_call_target="tpu_custom_call" | custom-call | tf_op jit(solution)/shard_map/cuts/pallas_call | solution.py:433
  183.2 2.1 collective-permute-start.4
  185.9 9.7 %all-to-all-done.7.code_ref = bf16[16,16,2176]{2,1,0:T(8,128)(2,1)S(1)} async-done(((bf16[16,16,2176]{2,1,0:T(8,128)(2,1)}), bf16[16,16,2176]{2,1,0:T(8,128)(2,1)S(1)}, u32[]{:S(2)}, u32[]{:S(2)}) %all-to-all-start.7) | async-done | bytes 1114144 | tf_op jit(solution)/shard_map/all_to_all | solution.py:223
  195.6 5.3 %collective-permute-done.3.refs_0_ = bf16[8,80,256]{2,1,0:T(8,128)(2,1)S(1)} collective-permute-done((bf16[8,80,256]{2,1,0:T(8,128)(2,1)S(1)}, bf16[8,80,256]{2,1,0:T(8,128)(2,1)S(1)}, u32[]{:S(2)}, u32[]{:S(2)}) %collective-permute-start.3) | collective-permute-done | bytes 327712 | tf_op jit(solution)/shard_map/ppermute | solution.py:506
  202.3 15.9 %all_to_all.55 = f32[16,32,256]{2,1,0:T(8,128)S(1)} all-to-all(f32[16,32,256]{2,1,0:T(8,128)S(1)} %bitcast.12), channel_id=1, replica_groups=mesh['yl'=2,'x'=4,'c'=2,'z'=4,'yh'=2] {'yl','x','yh'}, dimensions={0} | all-to-all | bytes 1048576 | tf_op jit(solution)/shard_map/all_to_all | solution.py:223
  218.9 4.5 %all-to-all-start.9 = ((f32[8,32,256]{2,1,0:T(8,128)}), f32[8,32,256]{2,1,0:T(8,128)S(1)}, u32[]{:S(2)}, u32[]{:S(2)}) async-start(f32[8,32,256]{2,1,0:T(8,128)} %broadcast_in_dim.2), calls=%async_computation.9 | async-start | bytes 524288 | tf_op jit(solution)/shard_map/all_to_all | solution.py:223
  223.5 2.1 decoded.1
  225.6 6.7 %all-to-all-done.9 = f32[8,32,256]{2,1,0:T(8,128)S(1)} async-done(((f32[8,32,256]{2,1,0:T(8,128)}), f32[8,32,256]{2,1,0:T(8,128)S(1)}, u32[]{:S(2)}, u32[]{:S(2)}) %all-to-all-start.9) | async-done | bytes 262176 | tf_op jit(solution)/shard_map/all_to_all | solution.py:223
  232.3 0.8 copy.5
  (36 shorter events, 5.1 us)
Async XLA Ops:
  7.2 0.9 copy-start.7
  9.2 21.1 %all-to-all-start = ((bf16[8,256,256]{2,1,0:T(8,128)(2,1)}), bf16[8,256,256]{2,1,0:T(8,128)(2,1)S(1)}, u32[]{:S(2)}, u32[]{:S(2)}) async-start(bf16[8,256,256]{2,1,0:T(8,128)(2,1)} %unit_copies.1), calls=%async_computation | async-start | bytes 2097152 | tf_op jit(solution)/shard_map/all_to_all | solution.py:223
  14.6 54.8 %all-gather.3.cloned.1.call-start = ((), (), s32[]{:S(2)}) async-start(), calls=%async_computation.10 | async-start | bytes 1179648 | tf_op jit(solution)/shard_map/all_gather | solution.py:530
  14.6 3.0 %copy-start.8 = (bf16[256,256]{1,0:T(8,128)(2,1)S(1)}, bf16[256,256]{1,0:T(8,128)(2,1)}, u32[]{:S(2)}) copy-start(bf16[256,256]{1,0:T(8,128)(2,1)} %param.4) | copy-start | bytes 393220
  30.3 2.7 %collective-permute-start = (bf16[8,256,256]{2,1,0:T(8,128)(2,1)S(1)}, bf16[8,256,256]{2,1,0:T(8,128)(2,1)S(1)}, u32[]{:S(2)}, u32[]{:S(2)}) collective-permute-start(bf16[8,256,256]{2,1,0:T(8,128)(2,1)S(1)} %all-to-all-done.refs_2_.refs_3_.refs_4_.near_ref), channel_id=1, source_target_pairs={{0,8},{8,0},{1,9},{9,1},{2,10},{10,2},{3,11},{11,3},{4,12},{12,4},... | collective-permute-start | bytes 3145736 | tf_op jit(solution)/shard_map/ppermute | solution.py:502
  33.1 1.2 copy-start
  34.3 35.1 %copy-start.1 = (bf16[2048,256]{1,0:T(8,128)(2,1)S(1)}, bf16[2048,256]{1,0:T(8,128)(2,1)}, u32[]{:S(2)}) copy-start(bf16[2048,256]{1,0:T(8,128)(2,1)} %get-tuple-element.30.refs_1_.refs_2_.protos_ref.refs_3_) | copy-start | bytes 3145732
  69.4 28.5 %collective-permute-start.1 = (bf16[8,256,256]{2,1,0:T(8,128)(2,1)}, bf16[8,256,256]{2,1,0:T(8,128)(2,1)}, u32[]{:S(2)}, u32[]{:S(2)}) collective-permute-start(bf16[8,256,256]{2,1,0:T(8,128)(2,1)} %bitcast.8), channel_id=1, source_target_pairs={{0,8},{8,0},{1,9},{9,1},{2,10},{10,2},{3,11},{11,3},{4,12},{12,4},... | collective-permute-start | bytes 3145736 | tf_op jit(solution)/shard_map/ppermute | solution.py:502
  93.7 11.9 %all-to-all-start.4 = ((f32[8,32,128]{2,1,0:T(8,128)}), f32[8,32,128]{2,1,0:T(8,128)S(1)}, u32[]{:S(2)}, u32[]{:S(2)}) async-start(f32[8,32,128]{2,1,0:T(8,128)} %hop.4), calls=%async_computation.4 | async-start | bytes 262144 | tf_op jit(solution)/shard_map/all_to_all | solution.py:223
  97.9 1.2 copy-start.2
  105.5 35.5 %copy-start.3 = (bf16[2048,256]{1,0:T(8,128)(2,1)S(1)}, bf16[2048,256]{1,0:T(8,128)(2,1)}, u32[]{:S(2)}) copy-start(bf16[2048,256]{1,0:T(8,128)(2,1)} %all-gather.3.cloned.1.call-done) | copy-start | bytes 3145732
  105.6 35.5 %copy-start.6 = (bf16[256,2048]{1,0:T(8,128)(2,1)S(1)}, bf16[256,2048]{1,0:T(8,128)(2,1)}, u32[]{:S(2)}) copy-start(bf16[256,2048]{1,0:T(8,128)(2,1)} %get-tuple-element.38.cols_ref) | copy-start | bytes 3145732
  162.6 1.3 copy-start.4
  163.9 14.5 %collective-permute-start.2 = (f32[8,256,256]{2,1,0:T(8,128)}, f32[8,256,256]{2,1,0:T(8,128)}, u32[]{:S(2)}, u32[]{:S(2)}) collective-permute-start(f32[8,256,256]{2,1,0:T(8,128)} %get-tuple-element.40), channel_id=1, source_target_pairs={{0,8},{8,0},{1,9},{9,1},{2,10},{10,2},{3,11},{11,3},{4,12},{12,4},... | collective-permute-start | bytes 6291464 | tf_op jit(solution)/shard_map/ppermute | solution.py:502
  174.7 20.9 %all-to-all-start.7 = ((bf16[16,16,2176]{2,1,0:T(8,128)(2,1)}), bf16[16,16,2176]{2,1,0:T(8,128)(2,1)S(1)}, u32[]{:S(2)}, u32[]{:S(2)}) async-start(bf16[16,16,2176]{2,1,0:T(8,128)(2,1)} %proto_part.1), calls=%async_computation.7 | async-start | bytes 2228224 | tf_op jit(solution)/shard_map/all_to_all | solution.py:223
  178.4 1.6 copy-start.5
  182.6 18.3 %collective-permute-start.3 = (bf16[8,80,256]{2,1,0:T(8,128)(2,1)S(1)}, bf16[8,80,256]{2,1,0:T(8,128)(2,1)S(1)}, u32[]{:S(2)}, u32[]{:S(2)}) collective-permute-start(bf16[8,80,256]{2,1,0:T(8,128)(2,1)S(1)} %get-tuple-element.42), channel_id=1, source_target_pairs={{0,2},{2,4},{4,6},{6,0},{1,3},{3,5},{5,7},{7,1},{8,10},{10,12},{12... | collective-permute-start | bytes 983048 | tf_op jit(solution)/shard_map/ppermute | solution.py:506
  183.2 17.7 %collective-permute-start.4 = (bf16[8,80,256]{2,1,0:T(8,128)(2,1)}, bf16[8,80,256]{2,1,0:T(8,128)(2,1)S(1)}, u32[]{:S(2)}, u32[]{:S(2)}) collective-permute-start(bf16[8,80,256]{2,1,0:T(8,128)(2,1)} %get-tuple-element.43), channel_id=1, source_target_pairs={{0,4},{2,6},{4,0},{6,2},{1,5},{3,7},{5,1},{7,3},{8,12},{10,14},{12... | collective-permute-start | bytes 983048 | tf_op jit(solution)/shard_map/ppermute | solution.py:506
  185.2 16.5 %collective-permute-start.5 = (bf16[8,80,256]{2,1,0:T(8,128)(2,1)S(1)}, bf16[8,80,256]{2,1,0:T(8,128)(2,1)S(1)}, u32[]{:S(2)}, u32[]{:S(2)}) collective-permute-start(bf16[8,80,256]{2,1,0:T(8,128)(2,1)S(1)} %get-tuple-element.44), channel_id=1, source_target_pairs={{0,6},{2,0},{4,2},{6,4},{1,7},{3,1},{5,3},{7,5},{8,14},{10,8},{12,... | collective-permute-start | bytes 983048 | tf_op jit(solution)/shard_map/ppermute | solution.py:506
  218.9 13.3 %all-to-all-start.9 = ((f32[8,32,256]{2,1,0:T(8,128)}), f32[8,32,256]{2,1,0:T(8,128)S(1)}, u32[]{:S(2)}, u32[]{:S(2)}) async-start(f32[8,32,256]{2,1,0:T(8,128)} %broadcast_in_dim.2), calls=%async_computation.9 | async-start | bytes 524288 | tf_op jit(solution)/shard_map/all_to_all | solution.py:223
Sparse Core Ops, SparseCore 0:
  30.4 38.7 all-gather.2

commit v3 on v2

--- a/solution.py
+++ b/solution.py
@@ -270,7 +270,7 @@
             ref[pair] = dot(cols_ref[...], diff[:, pl.ds(start, rows)])
         return carry
 
-    lax.fori_loop(0, pairs, one_pair, 0)
+    lax.fori_loop(0, pairs, one_pair, 0, unroll=4)
 
     def finish(step, carry):
         store(step).wait()

time: 241 us -> 240 us (level)
  no operation moved by 1% of the time
where the time goes in v3:
time: 240 us; the launch traced here: 239 us
  blocking collectives  83.7 us (35%)
  Pallas kernels  74 us (31%)
  waiting for transfers between devices  36.9 us (15%)
  starting transfers between devices  21.2 us (9%)
  between operations  14.2 us (6%)
  local copies, waits for them, and re-layouts  7.83 us (3%)
    all_to_all x6, blocking collectives, exchange(): return lax.all_to_all(parts, axes, 0, 0, tiled=True)  83.7 us
    all_to_all x4, waiting for transfers between devices, exchange(): return lax.all_to_all(parts, axes, 0, 0, tiled=True)  28.1 us
    pallas_call x3, Pallas kernels, sweep(): pl.pallas_call(functools.partial(sweep_kernel, copies, tile, parts is not...  26.3 us
    pallas_call x1, Pallas kernels, differences(): pl.pallas_call(functools.partial(diff_kernel, tile), in_specs=[smem()] +...  20.4 us
    all_to_all x4, starting transfers between devices, exchange(): return lax.all_to_all(parts, axes, 0, 0, tiled=True)  17.9 us
    pallas_call x1, Pallas kernels, proto_part(): pl.pallas_call(functools.partial(pgrad_kernel, tile), in_specs=[pl.BlockS...  10.8 us
    unnamed x19, local copies, waits for them, and re-layouts  7.1 us
    pallas_call x1, Pallas kernels, totals(): pl.pallas_call(functools.partial(totals_kernel, tile), in_specs=[smem()]...  6.4 us
  transfers between devices with their start and end apart: 11, of which 6 were waited for; matrix products, arithmetic and copies ran while one was open for 0% of the time, Pallas kernels for 18%

profile of v3, /device:TPU:0, one launch (start us, length us, event | category | flops | bytes accessed | tf_op | source)
XLA Modules:
  0.0 238.8 jit_solution(1759212261990911528)
XLA Ops:
  7.2 0.9 copy-done.7
  8.1 1.1 unit_copies.1
  9.2 5.4 %all-to-all-start = ((bf16[8,256,256]{2,1,0:T(8,128)(2,1)}), bf16[8,256,256]{2,1,0:T(8,128)(2,1)S(1)}, u32[]{:S(2)}, u32[]{:S(2)}) async-start(bf16[8,256,256]{2,1,0:T(8,128)(2,1)} %unit_copies.1), calls=%async_computation | async-start | bytes 2097152 | tf_op jit(solution)/shard_map/all_to_all | solution.py:223
  14.7 3.0 %unit_protos.1 = (bf16[256,2048]{1,0:T(8,128)(2,1)}, bf16[2048,256]{1,0:T(8,128)(2,1)}) custom-call(s32[1]{0:T(128)} %bitcast.2.place_ref, bf16[256,32768]{1,0:T(8,128)(2,1)} %weight_ref.1), custom_call_target="tpu_custom_call" | custom-call | flops 4194304 | bytes 20971520 | tf_op jit(solution)/shard_map/unit_protos/pallas_call | solution.py:484
  18.6 11.7 %all-to-all-done.refs_2_.refs_3_.refs_4_.near_ref = bf16[8,256,256]{2,1,0:T(8,128)(2,1)S(1)} async-done(((bf16[8,256,256]{2,1,0:T(8,128)(2,1)}), bf16[8,256,256]{2,1,0:T(8,128)(2,1)S(1)}, u32[]{:S(2)}, u32[]{:S(2)}) %all-to-all-start) | async-done | bytes 1048608 | tf_op jit(solution)/shard_map/all_to_all | solution.py:223
  30.4 2.6 %collective-permute-done.refs_3_.refs_4_.refs_5_.far_ref = bf16[8,256,256]{2,1,0:T(8,128)(2,1)S(1)} collective-permute-done((bf16[8,256,256]{2,1,0:T(8,128)(2,1)S(1)}, bf16[8,256,256]{2,1,0:T(8,128)(2,1)S(1)}, u32[]{:S(2)}, u32[]{:S(2)}) %collective-permute-start) | collective-permute-done | bytes 1048608 | tf_op jit(solution)/shard_map/ppermute | solution.py:502
  33.1 1.2 copy-done
  34.3 8.8 %sweep.3 = (f32[2048,128]{1,0:T(8,128)}, f32[16,32,128]{2,1,0:T(8,128)S(1)}) custom-call(s32[1]{0:T(128)} %bitcast.1.refs_0_.core_ref, bf16[2048,256]{1,0:T(8,128)(2,1)S(1)} %copy-done, bf16[8,256,256]{2,1,0:T(8,128)(2,1)S(1)} %all-to-all-done.refs_2_.refs_3_.refs_4_.near_ref, bf16[8,256,256]{2,1,0:T(8,128)(2,1)S(1)} %collective-permute-done.refs_3_.refs_4_.refs_5_.far_ref), custom_call_target="tpu_custom_call" | custom-call | tf_op jit(solution)/shard_map/sweep/pallas_call | solution.py:146
  43.1 14.8 %all_to_all.50.in_ref = f32[16,32,128]{2,1,0:T(8,128)S(1)} all-to-all(f32[16,32,128]{2,1,0:T(8,128)S(1)} %get-tuple-element.32), channel_id=1, replica_groups=mesh['yl'=2,'x'=4,'c'=2,'z'=4,'yh'=2] {'yl','x','yh'}, dimensions={0} | all-to-all | bytes 524288 | tf_op jit(solution)/shard_map/all_to_all | solution.py:223
  57.9 11.5 %all_to_all.51.refs_1_ = f32[8,32,128]{2,1,0:T(8,128)S(1)} all-to-all(f32[8,32,128]{2,1,0:T(8,128)S(1)} %hop.3), channel_id=1, replica_groups=mesh['yl'=2,'x'=4,'c'=2,'z'=4,'yh'=2] {'z','c'}, dimensions={0} | all-to-all | bytes 262144 | tf_op jit(solution)/shard_map/all_to_all | solution.py:223
  69.4 9.1 %sweep.4 = (f32[2048,128]{1,0:T(8,128)}, f32[16,32,128]{2,1,0:T(8,128)S(1)}) custom-call(s32[1]{0:T(128)} %bitcast.1.refs_0_.core_ref, f32[8,32,128]{2,1,0:T(8,128)S(1)} %all_to_all.51.refs_1_, bf16[2048,256]{1,0:T(8,128)(2,1)S(1)} %copy-done.1, bf16[8,256,256]{2,1,0:T(8,128)(2,1)S(1)} %all-to-all-done.refs_2_.refs_3_.refs_4_.near_ref, ...), custom_call_target="tpu_custom_call" | custom-call | tf_op jit(solution)/shard_map/sweep/pallas_call | solution.py:146
  78.5 14.5 %all_to_all.52.in_ref = f32[16,32,128]{2,1,0:T(8,128)S(1)} all-to-all(f32[16,32,128]{2,1,0:T(8,128)S(1)} %get-tuple-element.34), channel_id=1, replica_groups=mesh['yl'=2,'x'=4,'c'=2,'z'=4,'yh'=2] {'yl','x','yh'}, dimensions={0} | all-to-all | bytes 524288 | tf_op jit(solution)/shard_map/all_to_all | solution.py:223
  93.7 4.2 %all-to-all-start.4 = ((f32[8,32,128]{2,1,0:T(8,128)}), f32[8,32,128]{2,1,0:T(8,128)S(1)}, u32[]{:S(2)}, u32[]{:S(2)}) async-start(f32[8,32,128]{2,1,0:T(8,128)} %hop.4), calls=%async_computation.4 | async-start | bytes 262144 | tf_op jit(solution)/shard_map/all_to_all | solution.py:223
  97.9 1.2 copy-done.2
  99.1 6.4 %totals.1.refs_2_ = f32[32,128]{1,0:T(8,128)S(1)} custom-call(s32[1]{0:T(128)} %bitcast.1.refs_0_.core_ref, bf16[2048,256]{1,0:T(8,128)(2,1)S(1)} %copy-done.1, bf16[8,256,256]{2,1,0:T(8,128)(2,1)S(1)} %bitcast.10, bf16[8,256,256]{2,1,0:T(8,128)(2,1)} %collective-permute-done.1.far_ref.stud_far_ref), custom_call_target="tpu_custom_call" | custom-call | flops 4294967296 | bytes 4194304 | tf_op jit(solution)/shard_map/totals/pallas_call | solution.py:189
  105.6 8.4 %sweep.5 = (f32[2048,128]{1,0:T(8,128)S(1)}, f32[16,64,128]{2,1,0:T(8,128)S(1)}) custom-call(s32[1]{0:T(128)} %bitcast.1.refs_0_.core_ref, f32[8,32,128]{2,1,0:T(8,128)S(1)} %all-to-all-done.4.refs_1_, f32[32,128]{1,0:T(8,128)S(1)} %totals.1.refs_2_, bf16[2048,256]{1,0:T(8,128)(2,1)S(1)} %copy-done.1, ...), custom_call_target="tpu_custom_call" | custom-call | tf_op jit(solution)/shard_map/sweep/pallas_call | solution.py:146
  114.0 15.4 %all_to_all.53.in_ref = f32[16,64,128]{2,1,0:T(8,128)S(1)} all-to-all(f32[16,64,128]{2,1,0:T(8,128)S(1)} %get-tuple-element.36), channel_id=1, replica_groups=mesh['yl'=2,'x'=4,'c'=2,'z'=4,'yh'=2] {'yl','x','yh'}, dimensions={0} | all-to-all | bytes 1048576 | tf_op jit(solution)/shard_map/all_to_all | solution.py:223
  129.4 11.6 %all_to_all.54.parts_ref = f32[8,64,128]{2,1,0:T(8,128)S(1)} all-to-all(f32[8,64,128]{2,1,0:T(8,128)S(1)} %hop.5), channel_id=1, replica_groups=mesh['yl'=2,'x'=4,'c'=2,'z'=4,'yh'=2] {'z','c'}, dimensions={0} | all-to-all | bytes 524288 | tf_op jit(solution)/shard_map/all_to_all | solution.py:223
  141.0 20.4 %differences.1 = (bf16[2048,4096]{1,0:T(8,128)(2,1)}, f32[8,256,256]{2,1,0:T(8,128)S(1)}, f32[8,256,256]{2,1,0:T(8,128)}) custom-call(s32[1]{0:T(128)} %bitcast.1.refs_0_.core_ref, f32[8,64,128]{2,1,0:T(8,128)S(1)} %all_to_all.54.parts_ref, f32[2048,128]{1,0:T(8,128)S(1)} %get-tuple-element.37.col_ref, bf16[2048,256]{1,0:T(8,128)(2,1)S(1)} %copy-done.1, ...), custom_call_target="tpu_custom_call" | custom-call | tf_op jit(solution)/shard_map/differences/pallas_call | solution.py:287
  161.4 1.3 copy-done.4
  162.7 10.8 %proto_part.1 = bf16[16,16,2176]{2,1,0:T(8,128)(2,1)} custom-call(bf16[2048,4096]{1,0:T(8,128)(2,1)} %get-tuple-element.45.diff_ref, bf16[8,256,256]{2,1,0:T(8,128)(2,1)} %bitcast.9, bf16[8,256,256]{2,1,0:T(8,128)(2,1)} %collective-permute-done.1.far_ref.stud_far_ref), custom_call_target="tpu_custom_call" | custom-call | flops 4294967296 | bytes 20971520 | tf_op jit(solution)/shard_map/proto_part/pallas_call | solution.py:393
  173.5 3.7 %all-to-all-start.7 = ((bf16[16,16,2176]{2,1,0:T(8,128)(2,1)}), bf16[16,16,2176]{2,1,0:T(8,128)(2,1)S(1)}, u32[]{:S(2)}, u32[]{:S(2)}) async-start(bf16[16,16,2176]{2,1,0:T(8,128)(2,1)} %proto_part.1), calls=%async_computation.7 | async-start | bytes 2228224 | tf_op jit(solution)/shard_map/all_to_all | solution.py:223
  177.3 1.6 copy-done.5
  178.9 2.6 %cuts.1 = (f32[8,64,256]{2,1,0:T(8,128)S(1)}, bf16[8,80,256]{2,1,0:T(8,128)(2,1)S(1)}, bf16[8,80,256]{2,1,0:T(8,128)(2,1)}, bf16[8,80,256]{2,1,0:T(8,128)(2,1)S(1)}) custom-call(s32[1]{0:T(128)} %bitcast.level_ref, f32[8,256,256]{2,1,0:T(8,128)S(1)} %copy-done.5, f32[8,256,256]{2,1,0:T(8,128)} %collective-permute-done.2.given_ref), custom_call_target="tpu_custom_call" | custom-call | tf_op jit(solution)/shard_map/cuts/pallas_call | solution.py:433
  182.0 2.1 collective-permute-start.4
  184.7 9.7 %all-to-all-done.7.code_ref = bf16[16,16,2176]{2,1,0:T(8,128)(2,1)S(1)} async-done(((bf16[16,16,2176]{2,1,0:T(8,128)(2,1)}), bf16[16,16,2176]{2,1,0:T(8,128)(2,1)S(1)}, u32[]{:S(2)}, u32[]{:S(2)}) %all-to-all-start.7) | async-done | bytes 1114144 | tf_op jit(solution)/shard_map/all_to_all | solution.py:223
  194.4 5.3 %collective-permute-done.3.refs_0_ = bf16[8,80,256]{2,1,0:T(8,128)(2,1)S(1)} collective-permute-done((bf16[8,80,256]{2,1,0:T(8,128)(2,1)S(1)}, bf16[8,80,256]{2,1,0:T(8,128)(2,1)S(1)}, u32[]{:S(2)}, u32[]{:S(2)}) %collective-permute-start.3) | collective-permute-done | bytes 327712 | tf_op jit(solution)/shard_map/ppermute | solution.py:506
  201.1 15.9 %all_to_all.55 = f32[16,32,256]{2,1,0:T(8,128)S(1)} all-to-all(f32[16,32,256]{2,1,0:T(8,128)S(1)} %bitcast.12), channel_id=1, replica_groups=mesh['yl'=2,'x'=4,'c'=2,'z'=4,'yh'=2] {'yl','x','yh'}, dimensions={0} | all-to-all | bytes 1048576 | tf_op jit(solution)/shard_map/all_to_all | solution.py:223
  217.8 4.5 %all-to-all-start.9 = ((f32[8,32,256]{2,1,0:T(8,128)}), f32[8,32,256]{2,1,0:T(8,128)S(1)}, u32[]{:S(2)}, u32[]{:S(2)}) async-start(f32[8,32,256]{2,1,0:T(8,128)} %broadcast_in_dim.2), calls=%async_computation.9 | async-start | bytes 524288 | tf_op jit(solution)/shard_map/all_to_all | solution.py:223
  222.3 2.1 decoded.1
  224.4 6.7 %all-to-all-done.9 = f32[8,32,256]{2,1,0:T(8,128)S(1)} async-done(((f32[8,32,256]{2,1,0:T(8,128)}), f32[8,32,256]{2,1,0:T(8,128)S(1)}, u32[]{:S(2)}, u32[]{:S(2)}) %all-to-all-start.9) | async-done | bytes 262176 | tf_op jit(solution)/shard_map/all_to_all | solution.py:223
  231.1 0.8 copy.5
  (36 shorter events, 5.1 us)
Async XLA Ops:
  7.2 0.9 copy-start.7
  9.2 21.1 %all-to-all-start = ((bf16[8,256,256]{2,1,0:T(8,128)(2,1)}), bf16[8,256,256]{2,1,0:T(8,128)(2,1)S(1)}, u32[]{:S(2)}, u32[]{:S(2)}) async-start(bf16[8,256,256]{2,1,0:T(8,128)(2,1)} %unit_copies.1), calls=%async_computation | async-start | bytes 2097152 | tf_op jit(solution)/shard_map/all_to_all | solution.py:223
  14.6 54.8 %all-gather.3.cloned.1.call-start = ((), (), s32[]{:S(2)}) async-start(), calls=%async_computation.10 | async-start | bytes 1179648 | tf_op jit(solution)/shard_map/all_gather | solution.py:530
  14.6 3.0 %copy-start.8 = (bf16[256,256]{1,0:T(8,128)(2,1)S(1)}, bf16[256,256]{1,0:T(8,128)(2,1)}, u32[]{:S(2)}) copy-start(bf16[256,256]{1,0:T(8,128)(2,1)} %param.4) | copy-start | bytes 393220
  30.3 2.7 %collective-permute-start = (bf16[8,256,256]{2,1,0:T(8,128)(2,1)S(1)}, bf16[8,256,256]{2,1,0:T(8,128)(2,1)S(1)}, u32[]{:S(2)}, u32[]{:S(2)}) collective-permute-start(bf16[8,256,256]{2,1,0:T(8,128)(2,1)S(1)} %all-to-all-done.refs_2_.refs_3_.refs_4_.near_ref), channel_id=1, source_target_pairs={{0,8},{8,0},{1,9},{9,1},{2,10},{10,2},{3,11},{11,3},{4,12},{12,4},... | collective-permute-start | bytes 3145736 | tf_op jit(solution)/shard_map/ppermute | solution.py:502
  33.1 1.2 copy-start
  34.3 35.1 %copy-start.1 = (bf16[2048,256]{1,0:T(8,128)(2,1)S(1)}, bf16[2048,256]{1,0:T(8,128)(2,1)}, u32[]{:S(2)}) copy-start(bf16[2048,256]{1,0:T(8,128)(2,1)} %get-tuple-element.30.refs_1_.refs_2_.protos_ref.refs_3_) | copy-start | bytes 3145732
  69.4 28.5 %collective-permute-start.1 = (bf16[8,256,256]{2,1,0:T(8,128)(2,1)}, bf16[8,256,256]{2,1,0:T(8,128)(2,1)}, u32[]{:S(2)}, u32[]{:S(2)}) collective-permute-start(bf16[8,256,256]{2,1,0:T(8,128)(2,1)} %bitcast.8), channel_id=1, source_target_pairs={{0,8},{8,0},{1,9},{9,1},{2,10},{10,2},{3,11},{11,3},{4,12},{12,4},... | collective-permute-start | bytes 3145736 | tf_op jit(solution)/shard_map/ppermute | solution.py:502
  93.7 11.9 %all-to-all-start.4 = ((f32[8,32,128]{2,1,0:T(8,128)}), f32[8,32,128]{2,1,0:T(8,128)S(1)}, u32[]{:S(2)}, u32[]{:S(2)}) async-start(f32[8,32,128]{2,1,0:T(8,128)} %hop.4), calls=%async_computation.4 | async-start | bytes 262144 | tf_op jit(solution)/shard_map/all_to_all | solution.py:223
  97.9 1.2 copy-start.2
  105.5 35.5 %copy-start.3 = (bf16[2048,256]{1,0:T(8,128)(2,1)S(1)}, bf16[2048,256]{1,0:T(8,128)(2,1)}, u32[]{:S(2)}) copy-start(bf16[2048,256]{1,0:T(8,128)(2,1)} %all-gather.3.cloned.1.call-done) | copy-start | bytes 3145732
  105.6 35.5 %copy-start.6 = (bf16[256,2048]{1,0:T(8,128)(2,1)S(1)}, bf16[256,2048]{1,0:T(8,128)(2,1)}, u32[]{:S(2)}) copy-start(bf16[256,2048]{1,0:T(8,128)(2,1)} %get-tuple-element.38.cols_ref) | copy-start | bytes 3145732
  161.4 1.3 copy-start.4
  162.7 14.5 %collective-permute-start.2 = (f32[8,256,256]{2,1,0:T(8,128)}, f32[8,256,256]{2,1,0:T(8,128)}, u32[]{:S(2)}, u32[]{:S(2)}) collective-permute-start(f32[8,256,256]{2,1,0:T(8,128)} %get-tuple-element.40), channel_id=1, source_target_pairs={{0,8},{8,0},{1,9},{9,1},{2,10},{10,2},{3,11},{11,3},{4,12},{12,4},... | collective-permute-start | bytes 6291464 | tf_op jit(solution)/shard_map/ppermute | solution.py:502
  173.5 20.9 %all-to-all-start.7 = ((bf16[16,16,2176]{2,1,0:T(8,128)(2,1)}), bf16[16,16,2176]{2,1,0:T(8,128)(2,1)S(1)}, u32[]{:S(2)}, u32[]{:S(2)}) async-start(bf16[16,16,2176]{2,1,0:T(8,128)(2,1)} %proto_part.1), calls=%async_computation.7 | async-start | bytes 2228224 | tf_op jit(solution)/shard_map/all_to_all | solution.py:223
  177.3 1.6 copy-start.5
  181.5 18.3 %collective-permute-start.3 = (bf16[8,80,256]{2,1,0:T(8,128)(2,1)S(1)}, bf16[8,80,256]{2,1,0:T(8,128)(2,1)S(1)}, u32[]{:S(2)}, u32[]{:S(2)}) collective-permute-start(bf16[8,80,256]{2,1,0:T(8,128)(2,1)S(1)} %get-tuple-element.42), channel_id=1, source_target_pairs={{0,2},{2,4},{4,6},{6,0},{1,3},{3,5},{5,7},{7,1},{8,10},{10,12},{12... | collective-permute-start | bytes 983048 | tf_op jit(solution)/shard_map/ppermute | solution.py:506
  182.0 17.7 %collective-permute-start.4 = (bf16[8,80,256]{2,1,0:T(8,128)(2,1)}, bf16[8,80,256]{2,1,0:T(8,128)(2,1)S(1)}, u32[]{:S(2)}, u32[]{:S(2)}) collective-permute-start(bf16[8,80,256]{2,1,0:T(8,128)(2,1)} %get-tuple-element.43), channel_id=1, source_target_pairs={{0,4},{2,6},{4,0},{6,2},{1,5},{3,7},{5,1},{7,3},{8,12},{10,14},{12... | collective-permute-start | bytes 983048 | tf_op jit(solution)/shard_map/ppermute | solution.py:506
  184.1 16.5 %collective-permute-start.5 = (bf16[8,80,256]{2,1,0:T(8,128)(2,1)S(1)}, bf16[8,80,256]{2,1,0:T(8,128)(2,1)S(1)}, u32[]{:S(2)}, u32[]{:S(2)}) collective-permute-start(bf16[8,80,256]{2,1,0:T(8,128)(2,1)S(1)} %get-tuple-element.44), channel_id=1, source_target_pairs={{0,6},{2,0},{4,2},{6,4},{1,7},{3,1},{5,3},{7,5},{8,14},{10,8},{12,... | collective-permute-start | bytes 983048 | tf_op jit(solution)/shard_map/ppermute | solution.py:506
  217.8 13.3 %all-to-all-start.9 = ((f32[8,32,256]{2,1,0:T(8,128)}), f32[8,32,256]{2,1,0:T(8,128)S(1)}, u32[]{:S(2)}, u32[]{:S(2)}) async-start(f32[8,32,256]{2,1,0:T(8,128)} %broadcast_in_dim.2), calls=%async_computation.9 | async-start | bytes 524288 | tf_op jit(solution)/shard_map/all_to_all | solution.py:223
Sparse Core Ops, SparseCore 0:
  30.4 38.7 all-gather.2
